TPU v7x, 256 devices: a whole 4x4x8 slice. The times are simulated.
256 devices in a mesh: gx: 16 (over y_lo, x, core), gy: 16 (over y_hi, z).
Axes of the slice: x: 4, y: 4 (y_hi: 2, y_lo: 2; y = y_hi * 2 + y_lo), z: 8, core: 2. Of those that a mesh axis runs over, the one named last changes fastest.
Arguments:
- model_one: float32 [8, 256, 2048], P(None, 'gx', 'gy'), may hold values from -6 to 6
- model_two: float32 [8, 256, 2048], P(None, 'gx', 'gy'), may hold values from -6 to 6
- coupling_weight: float32 [8, 256, 2048], P(None, 'gx', 'gy'), may hold values from 0.2 to 2
- direction_one: float32 [10, 8, 256, 2048], P(None, None, 'gx', 'gy'), may hold values from -6 to 6
- direction_two: float32 [10, 8, 256, 2048], P(None, None, 'gx', 'gy'), may hold values from -6 to 6
Outputs:
- grad_one: float32 [8, 256, 2048], P(None, 'gx', 'gy')
- grad_two: float32 [8, 256, 2048], P(None, 'gx', 'gy')
- hess_one: float32 [10, 8, 256, 2048], P(None, None, 'gx', 'gy')
- hess_two: float32 [10, 8, 256, 2048], P(None, None, 'gx', 'gy')
All inputs are finite; a program needn't handle non-finite values.
Results may differ from a plain program's by a relative error of at most 0.00013.
Values sent between devices are 32-bit elements; how exact they have to be, the bound alone decides.
No kernel may reach another device: no remote copies, remote signals or barrier semaphores. Data moves between devices by JAX's collectives and lax.ppermute only.
A program may use at most 64 MiB of HBM per device.

v0:
```python
import jax
import jax.numpy as jnp
from jax import lax
from jax.sharding import PartitionSpec as P


def extended(cells, sides, width):
    for axis, dim in sides:
        count = lax.axis_size(axis)
        ends = count - 1
        head = lax.slice_in_dim(cells, 0, width, axis=dim)
        tail = lax.slice_in_dim(cells, cells.shape[dim] - width, cells.shape[dim], axis=dim)
        cells = jnp.concatenate(
            [
                lax.ppermute(tail, axis, [(i, (i + 1) % count) for i in range(ends)]),
                cells,
                lax.ppermute(head, axis, [((i + 1) % count, i) for i in range(ends)]),
            ],
            axis=dim,
        )
    return cells


def central(padded, along, length):

    def shifted(offset):
        return lax.slice_in_dim(padded, 2 + offset, 2 + offset + length, axis=along)

    return (8.0 * (shifted(1) - shifted(-1)) - (shifted(2) - shifted(-2))) / 12.0


def table_offsets(width_in, width_out):
    rows_in = lax.broadcasted_iota(jnp.int32, (width_in, width_out), 0)
    cols_out = lax.broadcasted_iota(jnp.int32, (width_in, width_out), 1)
    return rows_in - cols_out - 2


def band_matrix(width_in, width_out):
    spacing = table_offsets(width_in, width_out)
    near = jnp.where(spacing == 1, 8.0, jnp.where(spacing == -1, -8.0, 0.0))
    far = jnp.where(spacing == 2, -1.0, jnp.where(spacing == -2, 1.0, 0.0))
    return ((near + far) / 12.0).astype(jnp.float32)


def pick_matrix(width_in, width_out):
    return jnp.where(table_offsets(width_in, width_out) == 0, 1.0, 0.0).astype(jnp.float32)


def along_last(field, table):
    return jnp.matmul(
        field, table, precision=lax.Precision.HIGHEST, preferred_element_type=jnp.float32
    )


def layer_slope(interior):
    z_padded = jnp.pad(interior, ((0, 0), (2, 2), (0, 0), (0, 0)))
    return central(z_padded, 1, interior.shape[1])


def gradients(padded, extent_x, extent_y):
    width = padded.shape[3]
    columns = along_last(padded, pick_matrix(width, extent_y))
    slope_x = central(columns, 2, extent_x)
    slope_y = along_last(padded[:, :, 2:-2, :], band_matrix(width, extent_y))
    slope_z = layer_slope(columns[:, :, 2:-2, :])
    return (slope_x, slope_y, slope_z)


def cross_product(left, right):
    return (
        left[1] * right[2] - left[2] * right[1],
        left[2] * right[0] - left[0] * right[2],
        left[0] * right[1] - left[1] * right[0],
    )


def adjoint_fields(slopes, weight, directions):
    slope_one = tuple((part[0] for part in slopes))
    slope_two = tuple((part[1] for part in slopes))
    first_dirs = tuple((part[2 : 2 + directions] for part in slopes))
    second_dirs = tuple((part[2 + directions :] for part in slopes))
    coupled = cross_product(slope_one, slope_two)
    weighted = tuple((weight * part for part in coupled))
    adj_one = cross_product(slope_two, weighted)
    adj_two = cross_product(weighted, slope_one)
    left_term = cross_product(first_dirs, slope_two)
    right_term = cross_product(slope_one, second_dirs)
    reweighted = tuple((weight * (left_term[index] + right_term[index]) for index in range(3)))
    hess_left = cross_product(slope_two, reweighted)
    hess_right = cross_product(reweighted, slope_one)
    return tuple(
        (
            jnp.concatenate(
                [adj_one[index][None], adj_two[index][None], hess_left[index], hess_right[index]], 0
            )
            for index in range(3)
        )
    )


def shards(model_one, model_two, coupling_weight, direction_one, direction_two):
    directions = direction_one.shape[0]
    layers, rows_x, cols_y = model_one.shape
    fields = jnp.concatenate([model_one[None], model_two[None], direction_one, direction_two], 0)
    padded = extended(fields, (("gx", 2), ("gy", 3)), 2)
    slopes = gradients(padded, rows_x, cols_y)
    comp_x, comp_y, comp_z = adjoint_fields(slopes, coupling_weight, directions)
    comp_x = extended(comp_x, (("gx", 2),), 2)
    comp_y = extended(comp_y, (("gy", 3),), 2)
    width_y = cols_y + 4
    slope_comp_y = along_last(comp_y, band_matrix(width_y, cols_y))
    result = -(central(comp_x, 2, rows_x) + slope_comp_y + layer_slope(comp_z))
    return (result[0], result[1], result[2 : 2 + directions], result[2 + directions :])


def solution(mesh):
    return jax.shard_map(
        shards,
        mesh=mesh,
        in_specs=(
            P(None, "gx", "gy"),
            P(None, "gx", "gy"),
            P(None, "gx", "gy"),
            P(None, None, "gx", "gy"),
            P(None, None, "gx", "gy"),
        ),
        out_specs=(
            P(None, "gx", "gy"),
            P(None, "gx", "gy"),
            P(None, None, "gx", "gy"),
            P(None, None, "gx", "gy"),
        ),
        check_vma=False,
    )
```

profile of v0, /device:TPU:24, one launch (start us, length us, event | category | flops | bytes accessed | tf_op | source)
XLA Modules:
  0.0 100.6 jit_solution(1971055144085637600)
XLA Ops:
  0.6 0.0 copy-start
  0.6 0.0 copy-start.1
  0.7 1.5 %pad_maximum_fusion.11 = (f32[22,8,2,128]{3,2,1,0:T(2,128)S(1)}, f32[22,8,2,128]{3,2,1,0:T(2,128)S(1)}) fusion(f32[10,8,16,128]{3,2,1,0:T(8,128)} %param.9, f32[10,8,16,128]{3,2,1,0:T(8,128)} %param.8, f32[1,8,16,128]{3,2,1,0:T(8,128)} %bitcast.103, f32[1,8,16,128]{3,2,1,0:T(8,128)} %bitcast.106), kind=kLoop, calls=%fused_computation.68 | loop fusion | flops 270336 | bytes 1802240 | tf_op jit(solution)/shard_map/slice | solution.py:12
  2.2 4.3 %collective-permute-start.1 = (f32[22,8,2,128]{3,2,1,0:T(2,128)S(1)}, f32[22,8,2,128]{3,2,1,0:T(2,128)S(1)}, u32[]{:S(2)}, u32[]{:S(2)}) collective-permute-start(f32[22,8,2,128]{3,2,1,0:T(2,128)S(1)} %get-tuple-element.39), channel_id=1, source_target_pairs={{16,0},{32,16},{48,32},{64,48},{80,64},{96,80},{112,96},{128,112},... | collective-permute-start | bytes 540680 | tf_op jit(solution)/shard_map/ppermute | solution.py:17
  6.5 1.9 %collective-permute-start = (f32[22,8,2,128]{3,2,1,0:T(2,128)S(1)}, f32[22,8,2,128]{3,2,1,0:T(2,128)S(1)}, u32[]{:S(2)}, u32[]{:S(2)}) collective-permute-start(f32[22,8,2,128]{3,2,1,0:T(2,128)S(1)} %get-tuple-element.38), channel_id=1, source_target_pairs={{0,16},{16,32},{32,48},{48,64},{64,80},{80,96},{96,112},{112,128},... | collective-permute-start | bytes 540680 | tf_op jit(solution)/shard_map/ppermute | solution.py:15
  8.4 1.1 %collective-permute-done.1 = f32[22,8,2,128]{3,2,1,0:T(2,128)S(1)} collective-permute-done((f32[22,8,2,128]{3,2,1,0:T(2,128)S(1)}, f32[22,8,2,128]{3,2,1,0:T(2,128)S(1)}, u32[]{:S(2)}, u32[]{:S(2)}) %collective-permute-start.1) | collective-permute-done | bytes 180256 | tf_op jit(solution)/shard_map/ppermute | solution.py:17
  9.5 5.9 %collective-permute-done = f32[22,8,2,128]{3,2,1,0:T(2,128)S(1)} collective-permute-done((f32[22,8,2,128]{3,2,1,0:T(2,128)S(1)}, f32[22,8,2,128]{3,2,1,0:T(2,128)S(1)}, u32[]{:S(2)}, u32[]{:S(2)}) %collective-permute-start) | collective-permute-done | bytes 180256 | tf_op jit(solution)/shard_map/ppermute | solution.py:15
  15.4 0.0 copy-done.7
  15.4 0.7 copy-done.8
  16.1 0.0 copy-done
  16.1 0.0 copy-done.1
  16.1 1.3 %pad_maximum_fusion.1 = f32[22,8,20,128]{3,2,1,0:T(8,128)S(1)} fusion(f32[22,8,2,128]{3,2,1,0:T(2,128)S(1)} %collective-permute-done.1, f32[10,8,16,128]{3,2,1,0:T(8,128)S(1)} %copy-done, f32[10,8,16,128]{3,2,1,0:T(8,128)S(1)} %copy-done.1, f32[1,8,16,128]{3,2,1,0:T(8,128)} %bitcast.104, f32[1,8,16,128]{3,2,1,0:T(8,128)} %bitcast.107, ...), kind=kLoop, calls=%fused_computation.24 | loop fusion | flops 2252800 | bytes 3604480 | tf_op jit(solution)/shard_map/concatenate | solution.py:13
  17.3 2.1 %fusion.74 = (f32[22,8,20,2]{3,2,1,0:T(8,128)S(1)}, f32[22,8,20,2]{3,2,1,0:T(8,128)}) fusion(f32[22,8,20,128]{3,2,1,0:T(8,128)S(1)} %pad_maximum_fusion.1), kind=kLoop, calls=%fused_computation.127 | loop fusion | bytes 112640 | tf_op jit(solution)/shard_map/slice | solution.py:12
  19.5 3.4 %copy.16 = f32[22,8,20,2]{0,1,3,2:T(8,128)} copy(f32[22,8,20,2]{3,2,1,0:T(8,128)} %get-tuple-element.20) | data formatting | bytes 56320 | tf_op jit(solution)/shard_map/slice | solution.py:11
  22.9 8.1 %collective-permute-start.3 = (f32[22,8,20,2]{0,1,3,2:T(8,128)}, f32[22,8,20,2]{0,1,3,2:T(8,128)}, u32[]{:S(2)}, u32[]{:S(2)}) collective-permute-start(f32[22,8,20,2]{0,1,3,2:T(8,128)} %copy.16), channel_id=1, source_target_pairs={{1,0},{2,1},{3,2},{4,3},{5,4},{6,5},{7,6},{8,7},{9,8},{10,9},{11,1... | collective-permute-start | bytes 84488 | tf_op jit(solution)/shard_map/ppermute | solution.py:17
  31.1 2.0 %copy.15 = f32[22,8,20,2]{0,1,3,2:T(8,128)} copy(f32[22,8,20,2]{3,2,1,0:T(8,128)S(1)} %get-tuple-element.19) | data formatting | bytes 56320 | tf_op jit(solution)/shard_map/slice | solution.py:12
  33.0 2.0 %collective-permute-start.2 = (f32[22,8,20,2]{0,1,3,2:T(8,128)}, f32[22,8,20,2]{0,1,3,2:T(8,128)}, u32[]{:S(2)}, u32[]{:S(2)}) collective-permute-start(f32[22,8,20,2]{0,1,3,2:T(8,128)} %copy.15), channel_id=1, source_target_pairs={{0,1},{1,2},{2,3},{3,4},{4,5},{5,6},{6,7},{7,8},{8,9},{9,10},{10,1... | collective-permute-start | bytes 84488 | tf_op jit(solution)/shard_map/ppermute | solution.py:15
  35.1 0.0 collective-permute-done.3
  35.1 3.1 %copy.18 = f32[22,8,20,2]{3,2,1,0:T(8,128)S(1)} copy(f32[22,8,20,2]{0,1,3,2:T(8,128)} %collective-permute-done.3) | data formatting | bytes 56320 | tf_op jit(solution)/shard_map/ppermute | solution.py:17
  38.2 6.1 %collective-permute-done.2 = f32[22,8,20,2]{0,1,3,2:T(8,128)} collective-permute-done((f32[22,8,20,2]{0,1,3,2:T(8,128)}, f32[22,8,20,2]{0,1,3,2:T(8,128)}, u32[]{:S(2)}, u32[]{:S(2)}) %collective-permute-start.2) | collective-permute-done | bytes 28192 | tf_op jit(solution)/shard_map/ppermute | solution.py:15
  44.3 4.3 %copy.17 = f32[22,8,20,2]{3,2,1,0:T(8,128)} copy(f32[22,8,20,2]{0,1,3,2:T(8,128)} %collective-permute-done.2) | data formatting | bytes 56320 | tf_op jit(solution)/shard_map/ppermute | solution.py:15
  48.6 0.0 copy-done.9
  48.6 5.5 %pad_maximum_fusion = f32[22,8,20,132]{3,2,1,0:T(8,128)S(1)} fusion(f32[22,8,20,2]{3,2,1,0:T(8,128)S(1)} %copy.18, f32[22,8,2,128]{3,2,1,0:T(2,128)} %copy-done.7, f32[10,8,16,128]{3,2,1,0:T(8,128)S(1)} %copy-done, f32[10,8,16,128]{3,2,1,0:T(8,128)S(1)} %copy-done.1, f32[1,8,16,128]{3,2,1,0:T(8,128)S(1)} %bitcast.105, f32[1,8,16,128]{3,2,1,0:T(8,128)} %bitcast.108, ...), kind=kLoop, calls=%fused_computation | loop fusion | flops 3252480 | bytes 3717120 | tf_op jit(solution)/shard_map/concatenate | solution.py:13
  54.1 3.6 %fusion.34 = f32[22,8,20,128]{3,2,1,0:T(8,128)S(1)} fusion(f32[22,8,20,132]{3,2,1,0:T(8,128)S(1)} %pad_maximum_fusion), kind=kOutput, calls=%fused_computation.69 | convolution fusion | flops 713754624 | bytes 3660800 | tf_op jit(solution)/shard_map/dot_general | solution.py:50
  57.7 2.4 %fusion = f32[22,8,16,128]{3,2,1,0:T(8,128)S(1)} fusion(f32[22,8,20,132]{3,2,1,0:T(8,128)S(1)} %pad_maximum_fusion), kind=kOutput, calls=%fused_computation.3 | convolution fusion | flops 571152384 | bytes 4325376 | tf_op jit(solution)/shard_map/dot_general | solution.py:50
  60.2 0.6 fusion.30
  60.8 0.0 copy-start.6
  60.8 0.3 fusion.18
  61.1 0.5 copy-done.6
  61.7 0.0 copy-start.10
  61.7 0.5 multiply_subtract_fusion.3
  62.1 0.4 multiply_subtract_fusion.5
  62.5 0.0 copy-start.2
  62.6 1.3 %multiply_subtract_fusion.1 = (f32[10,8,16,128]{3,2,1,0:T(8,128)}, f32[10,8,16,128]{3,2,1,0:T(8,128)}, f32[10,8,16,128]{3,2,1,0:T(8,128)S(1)}) fusion(f32[10,8,16,128]{3,2,1,0:T(8,128)S(1)} %get-tuple-element.9, f32[10,8,16,128]{3,2,1,0:T(8,128)S(1)} %get-tuple-element.13, f32[8,16,128]{2,1,0:T(8,128)S(1)} %get-tuple-element.44, ...), kind=kLoop, calls=%fused_computation.53 | loop fusion | flops 1474560 | bytes 4259840 | tf_op jit(solution)/shard_map/sub | solution.py:73
  63.9 0.0 copy-start.12
  63.9 0.7 subtract_bitcast_fusion.1
  64.6 0.9 pad_maximum_fusion.7
  65.5 1.9 %collective-permute-start.4 = (f32[22,8,2,128]{3,2,1,0:T(2,128)}, f32[22,8,2,128]{3,2,1,0:T(2,128)}, u32[]{:S(2)}, u32[]{:S(2)}) collective-permute-start(f32[22,8,2,128]{3,2,1,0:T(2,128)} %get-tuple-element.30), channel_id=1, source_target_pairs={{16,0},{32,16},{48,32},{64,48},{80,64},{96,80},{112,96},{128,112},... | collective-permute-start | bytes 540680 | tf_op jit(solution)/shard_map/ppermute | solution.py:17
  67.4 2.4 %collective-permute-start.5 = (f32[22,8,2,128]{3,2,1,0:T(2,128)}, f32[22,8,2,128]{3,2,1,0:T(2,128)}, u32[]{:S(2)}, u32[]{:S(2)}) collective-permute-start(f32[22,8,2,128]{3,2,1,0:T(2,128)} %get-tuple-element.31), channel_id=1, source_target_pairs={{0,16},{16,32},{32,48},{48,64},{64,80},{80,96},{96,112},{112,128},... | collective-permute-start | bytes 540680 | tf_op jit(solution)/shard_map/ppermute | solution.py:15
  69.9 0.0 copy-done.10
  69.9 0.0 copy-done.2
  69.9 0.1 pad_maximum_fusion.3
  70.0 0.0 copy-done.12
  70.0 1.7 %fusion.76 = (f32[22,8,16,2]{3,2,1,0:T(8,128)S(1)}, f32[22,8,16,2]{3,2,1,0:T(8,128)}) fusion(f32[22,8,16,128]{3,2,1,0:T(8,128)S(1)} %pad_maximum_fusion.3), kind=kLoop, calls=%fused_computation.129 | loop fusion | bytes 90112 | tf_op jit(solution)/shard_map/slice | solution.py:12
  71.7 3.0 %copy.26 = f32[22,8,16,2]{0,2,3,1:T(8,128)} copy(f32[22,8,16,2]{3,2,1,0:T(8,128)} %get-tuple-element.27) | data formatting | bytes 45056 | tf_op jit(solution)/shard_map/slice | solution.py:11
  74.7 2.1 %collective-permute-start.7 = (f32[22,8,16,2]{0,2,3,1:T(8,128)}, f32[22,8,16,2]{0,2,3,1:T(8,128)}, u32[]{:S(2)}, u32[]{:S(2)}) collective-permute-start(f32[22,8,16,2]{0,2,3,1:T(8,128)} %copy.26), channel_id=1, source_target_pairs={{1,0},{2,1},{3,2},{4,3},{5,4},{6,5},{7,6},{8,7},{9,8},{10,9},{11,1... | collective-permute-start | bytes 67592 | tf_op jit(solution)/shard_map/ppermute | solution.py:17
  76.8 1.7 %copy.25 = f32[22,8,16,2]{0,2,3,1:T(8,128)} copy(f32[22,8,16,2]{3,2,1,0:T(8,128)S(1)} %get-tuple-element.26) | data formatting | bytes 45056 | tf_op jit(solution)/shard_map/slice | solution.py:12
  78.5 3.9 %collective-permute-start.6 = (f32[22,8,16,2]{0,2,3,1:T(8,128)}, f32[22,8,16,2]{0,2,3,1:T(8,128)}, u32[]{:S(2)}, u32[]{:S(2)}) collective-permute-start(f32[22,8,16,2]{0,2,3,1:T(8,128)} %copy.25), channel_id=1, source_target_pairs={{0,1},{1,2},{2,3},{3,4},{4,5},{5,6},{6,7},{7,8},{8,9},{9,10},{10,1... | collective-permute-start | bytes 67592 | tf_op jit(solution)/shard_map/ppermute | solution.py:15
  82.4 2.9 %select_maximum_fusion = f32[22,12,16,128]{3,2,1,0:T(8,128)} fusion(f32[10,8,16,128]{3,2,1,0:T(8,128)} %get-tuple-element.41, f32[10,8,16,128]{3,2,1,0:T(8,128)} %get-tuple-element.40, f32[1,8,16,128]{3,2,1,0:T(8,128)} %get-tuple-element.15, f32[1,8,16,128]{3,2,1,0:T(8,128)} %get-tuple-element.14), kind=kLoop, calls=%fused_computation.21 | loop fusion | flops 5406720 | bytes 3604480 | tf_op jit(solution)/shard_map/concatenate | solution.py:93
  85.4 0.0 collective-permute-done.7
  85.4 2.4 %copy.28 = f32[22,8,16,2]{3,2,1,0:T(8,128)S(1)} copy(f32[22,8,16,2]{0,2,3,1:T(8,128)} %collective-permute-done.7) | data formatting | bytes 45056 | tf_op jit(solution)/shard_map/ppermute | solution.py:17
  87.7 2.0 %collective-permute-done.6 = f32[22,8,16,2]{0,2,3,1:T(8,128)} collective-permute-done((f32[22,8,16,2]{0,2,3,1:T(8,128)}, f32[22,8,16,2]{0,2,3,1:T(8,128)}, u32[]{:S(2)}, u32[]{:S(2)}) %collective-permute-start.6) | collective-permute-done | bytes 22560 | tf_op jit(solution)/shard_map/ppermute | solution.py:15
  89.7 3.3 %copy.27 = f32[22,8,16,2]{3,2,1,0:T(8,128)} copy(f32[22,8,16,2]{0,2,3,1:T(8,128)} %collective-permute-done.6) | data formatting | bytes 45056 | tf_op jit(solution)/shard_map/ppermute | solution.py:15
  93.0 0.0 copy-start.13
  93.0 0.0 collective-permute-done.4
  93.1 0.0 collective-permute-done.5
  93.1 1.7 %pad_maximum_fusion.2 = (f32[22,8,18,128]{3,2,1,0:T(8,128)S(1)}, f32[22,8,18,128]{3,2,1,0:T(8,128)S(1)}) fusion(f32[22,8,2,128]{3,2,1,0:T(2,128)} %collective-permute-done.4, f32[10,8,16,128]{3,2,1,0:T(8,128)S(1)} %get-tuple-element.43, f32[10,8,16,128]{3,2,1,0:T(8,128)S(1)} %get-tuple-element.12, f32[1,8,16,128]{3,2,1,0:T(8,128)S(1)} %get-tuple-element.21, ...), kind=kLoop, calls=%fused_computation.25 | loop fusion | flops 3244032 | bytes 5046272 | tf_op jit(solution)/shard_map/concatenate | solution.py:13
  94.7 0.0 copy-done.3
  94.8 0.3 copy-done.4
  95.0 0.4 copy-done.5
  95.4 0.0 copy-done.11
  95.4 3.4 %fusion.23 = f32[22,8,16,128]{3,2,1,0:T(8,128)S(1)} fusion(f32[22,12,16,128]{3,2,1,0:T(8,128)S(1)} %copy-done.4, f32[22,8,18,128]{3,2,1,0:T(8,128)S(1)} %get-tuple-element.29, f32[22,8,18,128]{3,2,1,0:T(8,128)S(1)} %get-tuple-element.28, f32[22,8,16,2]{3,2,1,0:T(8,128)S(1)} %copy.28, f32[10,8,16,128]{3,2,1,0:T(8,128)S(1)} %copy-done.3, ...), kind=kOutput, calls=%fused_computation.37 | convolution fusion | flops 577696768 | bytes 14462976 | tf_op jit(solution)/shard_map/dot_general | solution.py:50
  98.8 0.7 slice_bitcast_fusion
  99.5 1.2 %fusion.75 = (f32[10,8,16,128]{3,2,1,0:T(8,128)}, f32[10,8,16,128]{3,2,1,0:T(8,128)}) fusion(f32[22,8,16,128]{3,2,1,0:T(8,128)S(1)} %fusion.23), kind=kLoop, calls=%fused_computation.128 | loop fusion | bytes 2621440 | tf_op jit(solution)/shard_map/slice | solution.py:113
  (12 shorter events, 0.1 us)
Async XLA Ops:
  0.6 15.4 %copy-start = (f32[10,8,16,128]{3,2,1,0:T(8,128)S(1)}, f32[10,8,16,128]{3,2,1,0:T(8,128)}, u32[]{:S(2)}) copy-start(f32[10,8,16,128]{3,2,1,0:T(8,128)} %param.9) | copy-start | bytes 1966084
  0.6 15.4 %copy-start.1 = (f32[10,8,16,128]{3,2,1,0:T(8,128)S(1)}, f32[10,8,16,128]{3,2,1,0:T(8,128)}, u32[]{:S(2)}) copy-start(f32[10,8,16,128]{3,2,1,0:T(8,128)} %param.8) | copy-start | bytes 1966084
  2.2 7.3 %collective-permute-start.1 = (f32[22,8,2,128]{3,2,1,0:T(2,128)S(1)}, f32[22,8,2,128]{3,2,1,0:T(2,128)S(1)}, u32[]{:S(2)}, u32[]{:S(2)}) collective-permute-start(f32[22,8,2,128]{3,2,1,0:T(2,128)S(1)} %get-tuple-element.39), channel_id=1, source_target_pairs={{16,0},{32,16},{48,32},{64,48},{80,64},{96,80},{112,96},{128,112},... | collective-permute-start | bytes 540680 | tf_op jit(solution)/shard_map/ppermute | solution.py:17
  6.5 8.9 %collective-permute-start = (f32[22,8,2,128]{3,2,1,0:T(2,128)S(1)}, f32[22,8,2,128]{3,2,1,0:T(2,128)S(1)}, u32[]{:S(2)}, u32[]{:S(2)}) collective-permute-start(f32[22,8,2,128]{3,2,1,0:T(2,128)S(1)} %get-tuple-element.38), channel_id=1, source_target_pairs={{0,16},{16,32},{32,48},{48,64},{64,80},{80,96},{96,112},{112,128},... | collective-permute-start | bytes 540680 | tf_op jit(solution)/shard_map/ppermute | solution.py:15
  9.5 5.9 %copy-start.7 = (f32[22,8,2,128]{3,2,1,0:T(2,128)}, f32[22,8,2,128]{3,2,1,0:T(2,128)S(1)}, u32[]{:S(2)}) copy-start(f32[22,8,2,128]{3,2,1,0:T(2,128)S(1)} %collective-permute-done.1) | copy-start | bytes 540676
  15.4 0.7 copy-start.8
  22.9 12.2 %collective-permute-start.3 = (f32[22,8,20,2]{0,1,3,2:T(8,128)}, f32[22,8,20,2]{0,1,3,2:T(8,128)}, u32[]{:S(2)}, u32[]{:S(2)}) collective-permute-start(f32[22,8,20,2]{0,1,3,2:T(8,128)} %copy.16), channel_id=1, source_target_pairs={{1,0},{2,1},{3,2},{4,3},{5,4},{6,5},{7,6},{8,7},{9,8},{10,9},{11,1... | collective-permute-start | bytes 84488 | tf_op jit(solution)/shard_map/ppermute | solution.py:17
  33.0 15.6 %copy-start.9 = (f32[8,16,128]{2,1,0:T(8,128)S(1)}, f32[8,16,128]{2,1,0:T(8,128)}, u32[]{:S(2)}) copy-start(f32[8,16,128]{2,1,0:T(8,128)} %param.6) | copy-start | bytes 196612
  33.0 11.3 %collective-permute-start.2 = (f32[22,8,20,2]{0,1,3,2:T(8,128)}, f32[22,8,20,2]{0,1,3,2:T(8,128)}, u32[]{:S(2)}, u32[]{:S(2)}) collective-permute-start(f32[22,8,20,2]{0,1,3,2:T(8,128)} %copy.15), channel_id=1, source_target_pairs={{0,1},{1,2},{2,3},{3,4},{4,5},{5,6},{6,7},{7,8},{8,9},{9,10},{10,1... | collective-permute-start | bytes 84488 | tf_op jit(solution)/shard_map/ppermute | solution.py:15
  60.8 0.8 copy-start.6
  61.7 8.2 %copy-start.10 = (f32[1,8,16,128]{3,2,1,0:T(8,128)}, f32[1,8,16,128]{3,2,1,0:T(8,128)S(1)}, u32[]{:S(2)}) copy-start(f32[1,8,16,128]{3,2,1,0:T(8,128)S(1)} %get-tuple-element.4) | copy-start | bytes 196612
  62.5 7.3 %copy-start.2 = (f32[10,8,16,128]{3,2,1,0:T(8,128)}, f32[10,8,16,128]{3,2,1,0:T(8,128)S(1)}, u32[]{:S(2)}) copy-start(f32[10,8,16,128]{3,2,1,0:T(8,128)S(1)} %get-tuple-element.42) | copy-start | bytes 1966084
  63.9 6.1 %copy-start.12 = (f32[1,8,16,128]{3,2,1,0:T(8,128)}, f32[1,8,16,128]{3,2,1,0:T(8,128)S(1)}, u32[]{:S(2)}) copy-start(f32[1,8,16,128]{3,2,1,0:T(8,128)S(1)} %get-tuple-element.16) | copy-start | bytes 196612
  65.5 27.5 %collective-permute-start.4 = (f32[22,8,2,128]{3,2,1,0:T(2,128)}, f32[22,8,2,128]{3,2,1,0:T(2,128)}, u32[]{:S(2)}, u32[]{:S(2)}) collective-permute-start(f32[22,8,2,128]{3,2,1,0:T(2,128)} %get-tuple-element.30), channel_id=1, source_target_pairs={{16,0},{32,16},{48,32},{64,48},{80,64},{96,80},{112,96},{128,112},... | collective-permute-start | bytes 540680 | tf_op jit(solution)/shard_map/ppermute | solution.py:17
  67.4 25.6 %collective-permute-start.5 = (f32[22,8,2,128]{3,2,1,0:T(2,128)}, f32[22,8,2,128]{3,2,1,0:T(2,128)}, u32[]{:S(2)}, u32[]{:S(2)}) collective-permute-start(f32[22,8,2,128]{3,2,1,0:T(2,128)} %get-tuple-element.31), channel_id=1, source_target_pairs={{0,16},{16,32},{32,48},{48,64},{64,80},{80,96},{96,112},{112,128},... | collective-permute-start | bytes 540680 | tf_op jit(solution)/shard_map/ppermute | solution.py:15
  74.7 10.7 %collective-permute-start.7 = (f32[22,8,16,2]{0,2,3,1:T(8,128)}, f32[22,8,16,2]{0,2,3,1:T(8,128)}, u32[]{:S(2)}, u32[]{:S(2)}) collective-permute-start(f32[22,8,16,2]{0,2,3,1:T(8,128)} %copy.26), channel_id=1, source_target_pairs={{1,0},{2,1},{3,2},{4,3},{5,4},{6,5},{7,6},{8,7},{9,8},{10,9},{11,1... | collective-permute-start | bytes 67592 | tf_op jit(solution)/shard_map/ppermute | solution.py:17
  78.5 11.2 %collective-permute-start.6 = (f32[22,8,16,2]{0,2,3,1:T(8,128)}, f32[22,8,16,2]{0,2,3,1:T(8,128)}, u32[]{:S(2)}, u32[]{:S(2)}) collective-permute-start(f32[22,8,16,2]{0,2,3,1:T(8,128)} %copy.25), channel_id=1, source_target_pairs={{0,1},{1,2},{2,3},{3,4},{4,5},{5,6},{6,7},{7,8},{8,9},{9,10},{10,1... | collective-permute-start | bytes 67592 | tf_op jit(solution)/shard_map/ppermute | solution.py:15
  93.0 1.7 %copy-start.3 = (f32[10,8,16,128]{3,2,1,0:T(8,128)S(1)}, f32[10,8,16,128]{3,2,1,0:T(8,128)}, u32[]{:S(2)}) copy-start(f32[10,8,16,128]{3,2,1,0:T(8,128)} %copy-done.2) | copy-start | bytes 1966084
  93.0 2.0 %copy-start.4 = (f32[22,12,16,128]{3,2,1,0:T(8,128)S(1)}, f32[22,12,16,128]{3,2,1,0:T(8,128)}, u32[]{:S(2)}) copy-start(f32[22,12,16,128]{3,2,1,0:T(8,128)} %select_maximum_fusion) | copy-start | bytes 6488068
  93.0 2.4 %copy-start.5 = (f32[22,8,16,2]{3,2,1,0:T(8,128)S(1)}, f32[22,8,16,2]{3,2,1,0:T(8,128)}, u32[]{:S(2)}) copy-start(f32[22,8,16,2]{3,2,1,0:T(8,128)} %copy.27) | copy-start | bytes 67588
  93.0 2.4 %copy-start.11 = (f32[1,8,16,128]{3,2,1,0:T(8,128)S(1)}, f32[1,8,16,128]{3,2,1,0:T(8,128)}, u32[]{:S(2)}) copy-start(f32[1,8,16,128]{3,2,1,0:T(8,128)} %copy-done.10) | copy-start | bytes 196612
  93.0 2.4 %copy-start.13 = (f32[1,8,16,128]{3,2,1,0:T(8,128)S(1)}, f32[1,8,16,128]{3,2,1,0:T(8,128)}, u32[]{:S(2)}) copy-start(f32[1,8,16,128]{3,2,1,0:T(8,128)} %copy-done.12) | copy-start | bytes 196612
where the time goes:
time: 101 us
  local copies, waits for them, and re-layouts  30.7 us (30%)
  starting transfers between devices  26.7 us (26%)
  other arithmetic  17.7 us (18%)
  waiting for transfers between devices  15.1 us (15%)
  matrix products  9.38 us (9%)
    ppermute x4, starting transfers between devices, extended(): lax.ppermute(head, axis, [((i + 1) % count, i) for i in range(ends)])  16.5 us
    ppermute x4, waiting for transfers between devices, extended(): lax.ppermute(tail, axis, [(i, (i + 1) % count) for i in range(ends)])  14 us
    ppermute x4, starting transfers between devices, extended(): lax.ppermute(tail, axis, [(i, (i + 1) % count) for i in range(ends)])  10.3 us
    dot_general x3, matrix products, along_last(): jnp.matmul(field, table, precision=lax.Precision.HIGHEST, preferred_eleme...  9.38 us
    concatenate x3, other arithmetic, extended(): jnp.concatenate([lax.ppermute(tail, axis, [(i, (i + 1) % count) for i in...  8.44 us
    ppermute x2, local copies, waits for them, and re-layouts, extended(): lax.ppermute(tail, axis, [(i, (i + 1) % count) for i in range(ends)])  7.59 us
    slice x4, local copies, waits for them, and re-layouts, extended(): lax.slice_in_dim(cells, cells.shape[dim] - width, cells.shape[dim], axis=...  7.53 us
    slice x2, local copies, waits for them, and re-layouts, extended(): head = lax.slice_in_dim(cells, 0, width, axis=dim)  6.4 us
  transfers between devices with their start and end apart: 8, of which 4 were waited for; matrix products, arithmetic and copies ran while one was open for 20% of the time, Pallas kernels for 0%

commit v1 on v0

v1 whole, which is shorter than its diff:
```python
import functools

import jax
import jax.numpy as jnp
from jax import lax
from jax.experimental import pallas as pl
from jax.experimental.pallas import tpu as pltpu
from jax.sharding import PartitionSpec as P

LAYERS = 8
ROWS = 16
EXT = 24
LANES = 128
MIB = 1024 * 1024
F32 = jnp.float32


def swap(count, first):
    pairs = []
    for low in range(first, count - 1, 2):
        pairs += [(low, low + 1), (low + 1, low)]
    return pairs


def shape(*dims):
    return jax.ShapeDtypeStruct(dims, F32)


def lane(dims):
    return lax.broadcasted_iota(jnp.int32, dims, len(dims) - 1)


def sub(dims):
    return lax.broadcasted_iota(jnp.int32, dims, len(dims) - 2)


def lroll(value, amount):
    return pltpu.roll(value, amount % LANES, axis=value.ndim - 1)


def sroll(value, amount):
    return pltpu.roll(value, amount % value.shape[-2], axis=value.ndim - 2)


def pack_body(dirs, m1, m2, w, d1, d2, xs, xb, xa, e1, e2):
    core = lax.rem(lax.axis_index("gx"), 2)
    tile = (8, LANES)
    upper = (sub(tile) >= 4).astype(jnp.int32)

    def edge_rows(one, two, tail, layer):
        start = pl.multiple_of(tail * 8, 8)
        first = one[layer, pl.ds(start, 8), :]
        second = two[layer, pl.ds(start, 8), :]
        return jnp.where(upper == tail, first, sroll(second, 4))

    a_tail = 1 - core
    b_tail = core

    def rows(index, one, two):
        for layer in range(LAYERS):
            xb[index, layer] = edge_rows(one, two, b_tail, layer)
            xa[index, layer] = edge_rows(one, two, a_tail, layer)

    block = lane((ROWS, LANES)) // 8
    for layer in range(LAYERS):
        first = jnp.zeros((ROWS, LANES), F32)
        second = jnp.zeros((ROWS, LANES), F32)
        for d in range(dirs):
            first = jnp.where(block == d, lroll(d1[d, layer], 8 * d + 4), first)
            second = jnp.where(block == d, lroll(d2[d, layer], 8 * d + 4), second)
        first = jnp.where(block == dirs, lroll(m1[layer], 8 * dirs + 4), first)
        first = jnp.where(block == dirs + 1, lroll(w[layer], 8 * dirs + 12), first)
        second = jnp.where(block == dirs + 1, lroll(m2[layer], 8 * dirs + 12), second)
        e1[layer] = first
        e2[layer] = second
    for layer in range(LAYERS):
        xs[layer] = edge_rows(e1, e2, b_tail, layer)
        xa[dirs + 2, layer] = edge_rows(e1, e2, a_tail, layer)

    @pl.loop(0, dirs)
    def _(d):
        rows(d, d1.at[d], d2.at[d])

    rows(dirs, m1, m2)
    rows(dirs + 1, w, w)


def join_rows(core, from_a, from_b):
    mask = ((sub(from_a.shape) < 4).astype(jnp.int32) + core) == 1
    return jnp.where(mask, from_a, from_b), sroll(jnp.where(mask, from_b, from_a), 4)


def edges_body(e1, e2, xa, xs, e1x, e2x, ya, yb):
    core = lax.rem(lax.axis_index("gx"), 2)
    side = lax.rem(lax.axis_index("gy"), 2)
    for layer in range(LAYERS):
        one, two = join_rows(core, xa[layer], xs[layer])
        one = jnp.concatenate([e1[layer], one], 0)
        two = jnp.concatenate([e2[layer], two], 0)
        e1x[layer] = one
        e2x[layer] = two
        low = (lane(one.shape) % 8) < 4
        tail = jnp.where(low, one, lroll(two, 4))
        head = jnp.where(low, lroll(two, -4), one)
        ya[layer] = jnp.where(side == 0, tail, head)
        yb[layer] = jnp.where(side == 0, head, tail)


def stencil(up2, up1, down1, down2):
    return 8.0 * (up1 - down1) - (up2 - down2)


def diff_x(value):
    return stencil(sroll(value, -2), sroll(value, -1), sroll(value, 1), sroll(value, 2))


def diff_y(value):
    return stencil(lroll(value, -2), lroll(value, -1), lroll(value, 1), lroll(value, 2))


def diff_z(ref, layer, rows=None):
    def at(offset):
        where = layer + offset
        if where < 0 or where >= LAYERS:
            return None
        return ref[where] if rows is None else ref[where, rows, :]

    total = None
    for offset, factor in ((1, 8.0), (-1, -8.0), (2, -1.0), (-2, 1.0)):
        part = at(offset)
        if part is None:
            continue
        if total is None:
            total = factor * part if factor != 1.0 else part
        elif factor == -1.0:
            total = total - part
        elif factor == 1.0:
            total = total + part
        elif at(-offset) is not None and offset == -1:
            total = 8.0 * (at(1) - part)
        else:
            total = total + factor * part
    return total


def cross(left, right):
    return (
        left[1] * right[2] - left[2] * right[1],
        left[2] * right[0] - left[0] * right[2],
        left[0] * right[1] - left[1] * right[0],
    )


def field_body(
    dirs, m1, m2, w, d1, d2, xa, xb, e1x, e2x, ya, yb,
    g1, g2, h1, h2,
    f_ext, g_ext, w_ext, s1, s2, dy1, dy2, hy1, hy2, hx, hz1, hz2, hsrc1, hsrc2, cor1, cor2, ax, ay, az,
):
    core = lax.rem(lax.axis_index("gx"), 2)
    side = lax.rem(lax.axis_index("gy"), 2)
    full = (EXT, LANES)
    lanes = lane(full)
    low = (lanes % 8) < 4
    edge = (lanes < 2) | (lanes >= 126)

    def load_ext(one, two, message, layer):
        tail1, tail2 = join_rows(core, xa[message, layer], xb[message, layer])
        f_ext[layer] = jnp.concatenate([one[layer], tail1], 0)
        g_ext[layer] = jnp.concatenate([two[layer], tail2], 0)

    for layer in range(LAYERS):
        from_a, from_b = ya[layer], yb[layer]
        left = jnp.where(side == 0, from_b, from_a)
        right = jnp.where(side == 0, from_a, from_b)
        left2, right2 = lroll(left, -4), lroll(right, 4)
        for src, left_i, right_i, halo, dy, hy in (
            (e1x, left, right, hsrc1, dy1, hy1),
            (e2x, left2, right2, hsrc2, dy2, hy2),
        ):
            own = src[layer]
            before = diff_y(jnp.where(low, left_i, own))
            after = diff_y(jnp.where(low, own, right_i))
            halo[layer] = jnp.where(low, left_i, right_i)
            dy[layer] = jnp.where(low, after, before)
            hy[layer] = jnp.where(low, before, after)

    fold = -1.0 / 20736.0
    for layer in range(LAYERS):
        load_ext(m1, m2, dirs, layer)
        wt, _ = join_rows(core, xa[dirs + 1, layer], xb[dirs + 1, layer])
        w_ext[layer] = jnp.concatenate([w[layer], wt], 0) * fold

    def slopes(ext, dy, amount, layer):
        value = ext[layer]
        slope_y = jnp.where(edge, pltpu.roll(dy[layer], amount, axis=1), diff_y(value))
        return diff_x(value), slope_y, diff_z(ext, layer)

    for layer in range(LAYERS):
        for ref, ext, dy, at in ((s1, f_ext, dy1, dirs), (s2, g_ext, dy2, dirs + 1)):
            for index, part in enumerate(slopes(ext, dy, (124 - 8 * at) % LANES, layer)):
                ref[index, layer] = part

    main = pl.ds(0, ROWS)
    block = lane((ROWS, LANES)) // 8
    kind = lane((ROWS, LANES)) % 8

    def spread(value, at):
        value = jnp.where(block == at, value, 0.0)
        for amount in (8, 16, 32, 64):
            value = value + lroll(value, amount)
        return value

    for layer in range(LAYERS):
        first = (diff_x(hsrc1[layer])[:ROWS], hy1[layer, main, :], diff_z(hsrc1, layer, main))
        second = (diff_x(hsrc2[layer])[:ROWS], hy2[layer, main, :], diff_z(hsrc2, layer, main))
        one = tuple(spread(part, dirs) for part in first)
        two = tuple(spread(part, dirs + 1) for part in second)
        weight = spread(hsrc1[layer, main, :], dirs + 1) * fold
        second = tuple(jnp.where(block == dirs, 0.0, part) for part in second)
        left_term = cross(first, two)
        right_term = cross(one, second)
        rw = tuple(weight * (left_term[i] + right_term[i]) for i in range(3))
        for value, cor in ((cross(two, rw)[1], cor1), (cross(rw, one)[1], cor2)):
            value_up1, value_up2 = lroll(value, -1), lroll(value, -2)
            value_down1, value_down2 = lroll(value, 1), lroll(value, 2)
            cor[layer] = jnp.where(
                kind == 2,
                -value_up2,
                jnp.where(
                    kind == 3,
                    8.0 * value_up1 - value_up2,
                    jnp.where(kind == 4, value_down2 - 8.0 * value_down1, value_down2),
                ),
            )

    lanes16 = lane((ROWS, LANES))
    edge16 = (lanes16 < 2) | (lanes16 >= 126)
    up1 = jnp.where(lanes16 < 127, 8.0, 0.0)
    down1 = jnp.where(lanes16 >= 1, 8.0, 0.0)
    up2 = jnp.where(lanes16 < 126, 1.0, 0.0)
    down2 = jnp.where(lanes16 >= 2, 1.0, 0.0)

    def pair(amount, outs, second_field):
        for layer in range(LAYERS):
            one = (s1[0, layer], s1[1, layer], s1[2, layer])
            two = (s2[0, layer], s2[1, layer], s2[2, layer])
            if second_field:
                perturbed = tuple(
                    p + q
                    for p, q in zip(
                        cross(slopes(f_ext, dy1, amount, layer), two), cross(one, slopes(g_ext, dy2, amount, layer))
                    )
                )
            else:
                perturbed = cross(one, two)
            weight = w_ext[layer]
            rw = tuple(weight * part for part in perturbed)
            for k, adj in ((0, cross(two, rw)), (1, cross(rw, one))):
                ax[k, layer] = adj[0]
                ay[k, layer] = adj[1][:ROWS]
                az[k, layer] = adj[2][:ROWS]
        for k, cor in ((0, cor1), (1, cor2)):
            for layer in range(LAYERS):
                y = ay[k, layer]
                part_y = (up1 * lroll(y, -1) - down1 * lroll(y, 1)) - (up2 * lroll(y, -2) - down2 * lroll(y, 2))
                part_y = part_y + jnp.where(edge16, pltpu.roll(cor[layer], amount, axis=1), 0.0)
                outs[k][layer] = diff_x(ax[k, layer])[:ROWS] + part_y + diff_z(az.at[k], layer)

    pair((124 - 8 * dirs) % LANES, (g1, g2), False)

    @pl.loop(0, dirs)
    def _(d):
        for layer in range(LAYERS):
            load_ext(d1.at[d], d2.at[d], d, layer)
        pair(124 - 8 * d, (h1.at[d], h2.at[d]), True)


def params():
    return pltpu.CompilerParams(vmem_limit_bytes=40 * MIB)


def shards(model_one, model_two, weight, direction_one, direction_two):
    dirs = direction_one.shape[0]
    tile = shape(LAYERS, ROWS, LANES)
    ext = shape(LAYERS, EXT, LANES)
    small = shape(LAYERS, 8, LANES)
    fields = (model_one, model_two, weight, direction_one, direction_two)
    xs, xb, xa, e1, e2 = pl.pallas_call(
        functools.partial(pack_body, dirs),
        out_shape=(small, shape(dirs + 2, LAYERS, 8, LANES), shape(dirs + 3, LAYERS, 8, LANES), tile, tile),
        compiler_params=params(),
        name="pack",
    )(*fields)
    count_x, count_y = lax.axis_size("gx"), lax.axis_size("gy")
    xs = lax.ppermute(xs, "gx", swap(count_x, 1))
    xb = lax.ppermute(xb, "gx", swap(count_x, 1))
    xa = lax.ppermute(xa, "gx", swap(count_x, 0))
    e1x, e2x, ya, yb = pl.pallas_call(
        edges_body,
        out_shape=(ext,) * 4,
        compiler_params=params(),
        name="edges",
    )(e1, e2, xa[dirs + 2], xs)
    yb = lax.ppermute(yb, "gy", swap(count_y, 1))
    ya = lax.ppermute(ya, "gy", swap(count_y, 0))
    scratch = lambda *dims: pltpu.VMEM(dims, F32)
    many = shape(dirs, LAYERS, ROWS, LANES)
    ext_s = scratch(LAYERS, EXT, LANES)
    ext_3 = scratch(3, LAYERS, EXT, LANES)
    tile_s = scratch(LAYERS, ROWS, LANES)
    tile_2 = scratch(2, LAYERS, ROWS, LANES)
    return pl.pallas_call(
        functools.partial(field_body, dirs),
        out_shape=(tile, tile, many, many),
        scratch_shapes=[
            ext_s, ext_s, ext_s, ext_3, ext_3, ext_s, ext_s, ext_s, ext_s, ext_s, ext_s, ext_s, ext_s, ext_s,
            tile_s, tile_s, scratch(2, LAYERS, EXT, LANES), tile_2, tile_2,
        ],
        compiler_params=params(),
        name="fields",
    )(*fields, xa, xb, e1x, e2x, ya, yb)


def solution(mesh):
    plane = P(None, "gx", "gy")
    stack = P(None, None, "gx", "gy")
    return jax.shard_map(
        shards,
        mesh=mesh,
        in_specs=(plane, plane, plane, stack, stack),
        out_specs=(plane, plane, stack, stack),
        check_vma=False,
    )
```

time: 101 us -> 50.5 us (0.50)
  local copies, waits for them, and re-layouts: 30.7 us -> 4.7 us
  Pallas kernels: 0 us -> 20.2 us
  other arithmetic: 17.7 us -> 0 us
  starting transfers between devices: 26.7 us -> 17 us
  matrix products: 9.38 us -> 0 us
  waiting for transfers between devices: 15.1 us -> 7.45 us
    pallas_call x0 -> x3, Pallas kernels: none -> 20.2 us  [the longest x1 19.4 us: shards(): pl.pallas_call(functools.partial(field_body, dirs), out_shape=(tile, tile...]
    slice x7 -> x0, local copies, waits for them, and re-layouts: 15.1 us -> none  [the longest x4 7.53 us: extended(): lax.slice_in_dim(cells, cells.shape[dim] - width, cells.shape[dim], axis=...]
    ppermute x4 -> x0, local copies, waits for them, and re-layouts: 13.1 us -> none  [the longest x2 7.59 us: extended(): lax.ppermute(tail, axis, [(i, (i + 1) % count) for i in range(ends)])]
    concatenate x5 -> x0, other arithmetic: 11.5 us -> none  [the longest x3 8.44 us: extended(): jnp.concatenate([lax.ppermute(tail, axis, [(i, (i + 1) % count) for i in...]
    ppermute x8 -> x5, starting transfers between devices: 26.7 us -> 17 us  [the longest x1 7.22 us: shards(): yb = lax.ppermute(yb, 'gy', swap(count_y, 1))]
    dot_general x3 -> x0, matrix products: 9.38 us -> none  [along_last(): jnp.matmul(field, table, precision=lax.Precision.HIGHEST, preferred_eleme...]
    ppermute x8 -> x5, waiting for transfers between devices: 15.1 us -> 7.45 us  [the longest x1 4.58 us: shards(): xs = lax.ppermute(xs, 'gx', swap(count_x, 1))]
    unnamed x28 -> x18, local copies, waits for them, and re-layouts: 1.89 us -> 4.7 us
  transfers between devices with their start and end apart: 8 -> 5, of which waited for: 4 -> 2; matrix products, arithmetic and copies ran while one was open for 20% -> 0% of each run, Pallas kernels for 0% -> 0%
where the time goes in v1:
time: 50.5 us; the launch traced here: 50.1 us
  Pallas kernels  20.2 us (40%)
  starting transfers between devices  17 us (34%)
  waiting for transfers between devices  7.45 us (15%)
  local copies, waits for them, and re-layouts  4.7 us (9%)
  between operations  0.74 us (1%)
    pallas_call x1, Pallas kernels, shards(): pl.pallas_call(functools.partial(field_body, dirs), out_shape=(tile, tile...  19.4 us
    ppermute x1, starting transfers between devices, shards(): yb = lax.ppermute(yb, 'gy', swap(count_y, 1))  7.22 us
    ppermute x1, starting transfers between devices, shards(): xb = lax.ppermute(xb, 'gx', swap(count_x, 1))  4.94 us
    unnamed x18, local copies, waits for them, and re-layouts  4.7 us
    ppermute x1, waiting for transfers between devices, shards(): xs = lax.ppermute(xs, 'gx', swap(count_x, 1))  4.58 us
    ppermute x1, waiting for transfers between devices, shards(): yb = lax.ppermute(yb, 'gy', swap(count_y, 1))  2.86 us
    ppermute x1, starting transfers between devices, shards(): xs = lax.ppermute(xs, 'gx', swap(count_x, 1))  2.74 us
    ppermute x1, starting transfers between devices, shards(): ya = lax.ppermute(ya, 'gy', swap(count_y, 0))  2 us
  transfers between devices with their start and end apart: 5, of which 2 were waited for; matrix products, arithmetic and copies ran while one was open for 0% of the time, Pallas kernels for 0%

profile of v1, /device:TPU:24, one launch (start us, length us, event | category | flops | bytes accessed | tf_op | source)
XLA Modules:
  0.0 50.1 jit_solution(12424261578430238551)
XLA Ops:
  0.6 0.0 copy-start
  0.6 1.1 %copy-done = f32[10,8,16,128]{3,2,1,0:T(8,128)S(1)} copy-done((f32[10,8,16,128]{3,2,1,0:T(8,128)S(1)}, f32[10,8,16,128]{3,2,1,0:T(8,128)}, u32[]{:S(2)}) %copy-start) | copy-done | bytes 655384
  1.7 0.0 copy-start.2
  1.7 1.1 %copy-done.2 = f32[10,8,16,128]{3,2,1,0:T(8,128)S(1)} copy-done((f32[10,8,16,128]{3,2,1,0:T(8,128)S(1)}, f32[10,8,16,128]{3,2,1,0:T(8,128)}, u32[]{:S(2)}) %copy-start.2) | copy-done | bytes 655384
  2.8 0.0 copy-start.3
  2.8 0.8 %copy-done.3 = f32[8,16,128]{2,1,0:T(8,128)S(1)} copy-done((f32[8,16,128]{2,1,0:T(8,128)S(1)}, f32[8,16,128]{2,1,0:T(8,128)}, u32[]{:S(2)}) %copy-start.3) | copy-done | bytes 65560
  3.6 0.0 copy-start.5
  3.6 0.8 %copy-done.5 = f32[8,16,128]{2,1,0:T(8,128)S(1)} copy-done((f32[8,16,128]{2,1,0:T(8,128)S(1)}, f32[8,16,128]{2,1,0:T(8,128)}, u32[]{:S(2)}) %copy-start.5) | copy-done | bytes 65560
  4.5 0.0 copy-start.7
  4.5 0.8 %copy-done.7 = f32[8,16,128]{2,1,0:T(8,128)S(1)} copy-done((f32[8,16,128]{2,1,0:T(8,128)S(1)}, f32[8,16,128]{2,1,0:T(8,128)}, u32[]{:S(2)}) %copy-start.7) | copy-done | bytes 65560
  5.3 0.0 copy-start.1
  5.3 0.6 %pack.1 = (f32[8,8,128]{2,1,0:T(8,128)S(1)}, f32[12,8,8,128]{3,2,1,0:T(8,128)S(1)}, f32[13,8,8,128]{3,2,1,0:T(8,128)S(1)}, f32[8,16,128]{2,1,0:T(8,128)S(1)}, f32[8,16,128]{2,1,0:T(8,128)S(1)}) custom-call(f32[8,16,128]{2,1,0:T(8,128)S(1)} %copy-done.3, f32[8,16,128]{2,1,0:T(8,128)S(1)} %copy-done.5, f32[8,16,128]{2,1,0:T(8,128)S(1)} %copy-done.7, ...), custom_call_target="tpu_custom_call" | custom-call | tf_op jit(solution)/shard_map/pack/pallas_call | solution.py:288
  6.0 0.1 collective-permute-start
  6.1 4.9 %collective-permute-start.1 = (f32[12,8,8,128]{3,2,1,0:T(8,128)S(1)}, f32[12,8,8,128]{3,2,1,0:T(8,128)S(1)}, u32[]{:S(2)}, u32[]{:S(2)}) collective-permute-start(f32[12,8,8,128]{3,2,1,0:T(8,128)S(1)} %get-tuple-element.14), channel_id=1, source_target_pairs={{16,32},{32,16},{48,64},{64,48},{80,96},{96,80},{112,128},{128,112... | collective-permute-start | bytes 1179656 | tf_op jit(solution)/shard_map/ppermute | solution.py:296
  11.0 2.7 %collective-permute-start.2 = (f32[8,8,128]{2,1,0:T(8,128)S(1)}, f32[8,8,128]{2,1,0:T(8,128)S(1)}, u32[]{:S(2)}, u32[]{:S(2)}) collective-permute-start(f32[8,8,128]{2,1,0:T(8,128)S(1)} %get-tuple-element.17), channel_id=1, source_target_pairs={{16,32},{32,16},{48,64},{64,48},{80,96},{96,80},{112,128},{128,112... | collective-permute-start | bytes 98312 | tf_op jit(solution)/shard_map/ppermute | solution.py:295
  13.7 0.0 collective-permute-done.xa
  13.8 4.6 %collective-permute-done.2.xs = f32[8,8,128]{2,1,0:T(8,128)S(1)} collective-permute-done((f32[8,8,128]{2,1,0:T(8,128)S(1)}, f32[8,8,128]{2,1,0:T(8,128)S(1)}, u32[]{:S(2)}, u32[]{:S(2)}) %collective-permute-start.2) | collective-permute-done | bytes 32800 | tf_op jit(solution)/shard_map/ppermute | solution.py:295
  18.3 0.0 copy-start.4
  18.4 0.0 copy-start.6
  18.4 0.0 copy-start.8
  18.4 0.1 edges.1
  18.5 2.0 %collective-permute-start.3 = (f32[8,24,128]{2,1,0:T(8,128)S(1)}, f32[8,24,128]{2,1,0:T(8,128)S(1)}, u32[]{:S(2)}, u32[]{:S(2)}) collective-permute-start(f32[8,24,128]{2,1,0:T(8,128)S(1)} %get-tuple-element.20), channel_id=1, source_target_pairs={{0,1},{1,0},{2,3},{3,2},{4,5},{5,4},{6,7},{7,6},{8,9},{9,8},{10,11... | collective-permute-start | bytes 294920 | tf_op jit(solution)/shard_map/ppermute | solution.py:305
  20.5 7.2 %collective-permute-start.4 = (f32[8,24,128]{2,1,0:T(8,128)S(1)}, f32[8,24,128]{2,1,0:T(8,128)S(1)}, u32[]{:S(2)}, u32[]{:S(2)}) collective-permute-start(f32[8,24,128]{2,1,0:T(8,128)S(1)} %get-tuple-element.21), channel_id=1, source_target_pairs={{1,2},{2,1},{3,4},{4,3},{5,6},{6,5},{7,8},{8,7},{9,10},{10,9},{11,... | collective-permute-start | bytes 294920 | tf_op jit(solution)/shard_map/ppermute | solution.py:304
  27.7 0.0 collective-permute-done.1.xb
  27.7 0.0 collective-permute-done.3.ya
  27.7 2.9 %collective-permute-done.4.yb = f32[8,24,128]{2,1,0:T(8,128)S(1)} collective-permute-done((f32[8,24,128]{2,1,0:T(8,128)S(1)}, f32[8,24,128]{2,1,0:T(8,128)S(1)}, u32[]{:S(2)}, u32[]{:S(2)}) %collective-permute-start.4) | collective-permute-done | bytes 98336 | tf_op jit(solution)/shard_map/ppermute | solution.py:304
  30.6 0.0 copy-done.1
  30.6 0.0 copy-done.4
  30.6 0.0 copy-done.6
  30.6 0.0 copy-done.8
  30.6 19.4 %fields.1 = (f32[8,16,128]{2,1,0:T(8,128)}, f32[8,16,128]{2,1,0:T(8,128)}, f32[10,8,16,128]{3,2,1,0:T(8,128)}, f32[10,8,16,128]{3,2,1,0:T(8,128)}) custom-call(f32[8,16,128]{2,1,0:T(8,128)S(1)} %copy-done.4, f32[8,16,128]{2,1,0:T(8,128)S(1)} %copy-done.6, f32[8,16,128]{2,1,0:T(8,128)S(1)} %copy-done.8, f32[10,8,16,128]{3,2,1,0:T(8,128)S(1)} %copy-done.1, ...), custom_call_target="tpu_custom_call" | custom-call | tf_op jit(solution)/shard_map/fields/pallas_call | solution.py:312
  (1 shorter events, 0.0 us)
Async XLA Ops:
  0.6 1.1 %copy-start = (f32[10,8,16,128]{3,2,1,0:T(8,128)S(1)}, f32[10,8,16,128]{3,2,1,0:T(8,128)}, u32[]{:S(2)}) copy-start(f32[10,8,16,128]{3,2,1,0:T(8,128)} %d1.3) | copy-start | bytes 1966084
  1.7 1.1 %copy-start.2 = (f32[10,8,16,128]{3,2,1,0:T(8,128)S(1)}, f32[10,8,16,128]{3,2,1,0:T(8,128)}, u32[]{:S(2)}) copy-start(f32[10,8,16,128]{3,2,1,0:T(8,128)} %d2.3) | copy-start | bytes 1966084
  2.8 0.8 %copy-start.3 = (f32[8,16,128]{2,1,0:T(8,128)S(1)}, f32[8,16,128]{2,1,0:T(8,128)}, u32[]{:S(2)}) copy-start(f32[8,16,128]{2,1,0:T(8,128)} %m1.3) | copy-start | bytes 196612
  3.6 0.8 %copy-start.5 = (f32[8,16,128]{2,1,0:T(8,128)S(1)}, f32[8,16,128]{2,1,0:T(8,128)}, u32[]{:S(2)}) copy-start(f32[8,16,128]{2,1,0:T(8,128)} %m2.3) | copy-start | bytes 196612
  4.5 0.8 %copy-start.7 = (f32[8,16,128]{2,1,0:T(8,128)S(1)}, f32[8,16,128]{2,1,0:T(8,128)}, u32[]{:S(2)}) copy-start(f32[8,16,128]{2,1,0:T(8,128)} %w.3) | copy-start | bytes 196612
  5.3 25.3 %copy-start.1 = (f32[10,8,16,128]{3,2,1,0:T(8,128)S(1)}, f32[10,8,16,128]{3,2,1,0:T(8,128)}, u32[]{:S(2)}) copy-start(f32[10,8,16,128]{3,2,1,0:T(8,128)} %d1.3) | copy-start | bytes 1966084
  6.0 7.8 %collective-permute-start = (f32[13,8,8,128]{3,2,1,0:T(8,128)S(1)}, f32[13,8,8,128]{3,2,1,0:T(8,128)S(1)}, u32[]{:S(2)}, u32[]{:S(2)}) collective-permute-start(f32[13,8,8,128]{3,2,1,0:T(8,128)S(1)} %get-tuple-element.13), channel_id=1, source_target_pairs={{0,16},{16,0},{32,48},{48,32},{64,80},{80,64},{96,112},{112,96},{1... | collective-permute-start | bytes 1277960 | tf_op jit(solution)/shard_map/ppermute | solution.py:297
  6.1 21.7 %collective-permute-start.1 = (f32[12,8,8,128]{3,2,1,0:T(8,128)S(1)}, f32[12,8,8,128]{3,2,1,0:T(8,128)S(1)}, u32[]{:S(2)}, u32[]{:S(2)}) collective-permute-start(f32[12,8,8,128]{3,2,1,0:T(8,128)S(1)} %get-tuple-element.14), channel_id=1, source_target_pairs={{16,32},{32,16},{48,64},{64,48},{80,96},{96,80},{112,128},{128,112... | collective-permute-start | bytes 1179656 | tf_op jit(solution)/shard_map/ppermute | solution.py:296
  11.0 7.3 %collective-permute-start.2 = (f32[8,8,128]{2,1,0:T(8,128)S(1)}, f32[8,8,128]{2,1,0:T(8,128)S(1)}, u32[]{:S(2)}, u32[]{:S(2)}) collective-permute-start(f32[8,8,128]{2,1,0:T(8,128)S(1)} %get-tuple-element.17), channel_id=1, source_target_pairs={{16,32},{32,16},{48,64},{64,48},{80,96},{96,80},{112,128},{128,112... | collective-permute-start | bytes 98312 | tf_op jit(solution)/shard_map/ppermute | solution.py:295
  18.3 12.3 %copy-start.4 = (f32[8,16,128]{2,1,0:T(8,128)S(1)}, f32[8,16,128]{2,1,0:T(8,128)}, u32[]{:S(2)}) copy-start(f32[8,16,128]{2,1,0:T(8,128)} %m1.3) | copy-start | bytes 196612
  18.4 12.3 %copy-start.6 = (f32[8,16,128]{2,1,0:T(8,128)S(1)}, f32[8,16,128]{2,1,0:T(8,128)}, u32[]{:S(2)}) copy-start(f32[8,16,128]{2,1,0:T(8,128)} %m2.3) | copy-start | bytes 196612
  18.4 12.3 %copy-start.8 = (f32[8,16,128]{2,1,0:T(8,128)S(1)}, f32[8,16,128]{2,1,0:T(8,128)}, u32[]{:S(2)}) copy-start(f32[8,16,128]{2,1,0:T(8,128)} %w.3) | copy-start | bytes 196612
  18.5 9.2 %collective-permute-start.3 = (f32[8,24,128]{2,1,0:T(8,128)S(1)}, f32[8,24,128]{2,1,0:T(8,128)S(1)}, u32[]{:S(2)}, u32[]{:S(2)}) collective-permute-start(f32[8,24,128]{2,1,0:T(8,128)S(1)} %get-tuple-element.20), channel_id=1, source_target_pairs={{0,1},{1,0},{2,3},{3,2},{4,5},{5,4},{6,7},{7,6},{8,9},{9,8},{10,11... | collective-permute-start | bytes 294920 | tf_op jit(solution)/shard_map/ppermute | solution.py:305
  20.5 10.1 %collective-permute-start.4 = (f32[8,24,128]{2,1,0:T(8,128)S(1)}, f32[8,24,128]{2,1,0:T(8,128)S(1)}, u32[]{:S(2)}, u32[]{:S(2)}) collective-permute-start(f32[8,24,128]{2,1,0:T(8,128)S(1)} %get-tuple-element.21), channel_id=1, source_target_pairs={{1,2},{2,1},{3,4},{4,3},{5,6},{6,5},{7,8},{8,7},{9,10},{10,9},{11,... | collective-permute-start | bytes 294920 | tf_op jit(solution)/shard_map/ppermute | solution.py:304

commit v2 on v1

v2 whole, which is shorter than its diff:
```python
import functools

import jax
import jax.numpy as jnp
from jax import lax
from jax.experimental import pallas as pl
from jax.experimental.pallas import tpu as pltpu
from jax.sharding import PartitionSpec as P

LAYERS = 8
ROWS = 16
EXT = 24
LANES = 128
MIB = 1024 * 1024
F32 = jnp.float32


def swap(count, first):
    pairs = []
    for low in range(first, count - 1, 2):
        pairs += [(low, low + 1), (low + 1, low)]
    return pairs


def shape(*dims):
    return jax.ShapeDtypeStruct(dims, F32)


def scratch(*dims):
    return pltpu.VMEM(dims, F32)


def half(*dims):
    return pltpu.VMEM(dims, jnp.bfloat16)


def lane(dims):
    return lax.broadcasted_iota(jnp.int32, dims, len(dims) - 1)


def sub(dims):
    return lax.broadcasted_iota(jnp.int32, dims, len(dims) - 2)


def lroll(value, amount):
    return pltpu.roll(value, amount % LANES, axis=value.ndim - 1)


def sroll(value, amount):
    return pltpu.roll(value, amount % value.shape[-2], axis=value.ndim - 2)


def edge_rows(one, two, tail, layer):
    upper = (sub((8, LANES)) >= 4).astype(jnp.int32)
    start = pl.multiple_of(tail * 8, 8)
    first = one[layer, pl.ds(start, 8), :]
    second = two[layer, pl.ds(start, 8), :]
    return jnp.where(upper == tail, first, sroll(second, 4))


def message_rows(dirs, tail, out, m1, m2, w, d1, d2):
    def rows(index, one, two):
        for layer in range(LAYERS):
            out[index, layer] = edge_rows(one, two, tail, layer)

    for d in range(dirs):
        rows(d, d1.at[d], d2.at[d])
    rows(dirs, m1, m2)
    rows(dirs + 1, w, w)


def far_body(dirs, first, m1, m2, w, d1, d2, xb):
    message_rows(dirs, lax.rem(lax.axis_index("gx"), 2), xb, m1, m2, w, d1, d2)


def pack_body(dirs, first, m1, m2, w, d1, d2, xs, xa, e1, e2):
    core = lax.rem(lax.axis_index("gx"), 2)
    a_tail = 1 - core
    b_tail = core

    block = lane((ROWS, LANES)) // 8
    for layer in range(LAYERS):
        first = jnp.zeros((ROWS, LANES), F32)
        second = jnp.zeros((ROWS, LANES), F32)
        for d in range(dirs):
            first = jnp.where(block == d, lroll(d1[d, layer], 8 * d + 4), first)
            second = jnp.where(block == d, lroll(d2[d, layer], 8 * d + 4), second)
        first = jnp.where(block == dirs, lroll(m1[layer], 8 * dirs + 4), first)
        first = jnp.where(block == dirs + 1, lroll(w[layer], 8 * dirs + 12), first)
        second = jnp.where(block == dirs + 1, lroll(m2[layer], 8 * dirs + 12), second)
        e1[layer] = first
        e2[layer] = second
    for layer in range(LAYERS):
        xs[layer] = edge_rows(e1, e2, b_tail, layer)
        xa[dirs + 2, layer] = edge_rows(e1, e2, a_tail, layer)

    message_rows(dirs, a_tail, xa, m1, m2, w, d1, d2)


def join_rows(core, from_a, from_b):
    mask = ((sub(from_a.shape) < 4).astype(jnp.int32) + core) == 1
    return jnp.where(mask, from_a, from_b), sroll(jnp.where(mask, from_b, from_a), 4)


def edges_body(e1, e2, xa, xs, e1x, e2x, ya, yb):
    core = lax.rem(lax.axis_index("gx"), 2)
    side = lax.rem(lax.axis_index("gy"), 2)
    for layer in range(LAYERS):
        one, two = join_rows(core, xa[layer], xs[layer])
        one = jnp.concatenate([e1[layer], one], 0)
        two = jnp.concatenate([e2[layer], two], 0)
        e1x[layer] = one
        e2x[layer] = two
        low = (lane(one.shape) % 8) < 4
        tail = jnp.where(low, one, lroll(two, 4))
        head = jnp.where(low, lroll(two, -4), one)
        ya[layer] = jnp.where(side == 0, tail, head)
        yb[layer] = jnp.where(side == 0, head, tail)


def stencil(up2, up1, down1, down2):
    return 8.0 * (up1 - down1) - (up2 - down2)


def diff_x(value):
    return stencil(sroll(value, -2), sroll(value, -1), sroll(value, 1), sroll(value, 2))


def diff_y(value):
    return stencil(lroll(value, -2), lroll(value, -1), lroll(value, 1), lroll(value, 2))


def diff_z(ref, layer, rows=None):
    def at(offset):
        where = layer + offset
        if where < 0 or where >= LAYERS:
            return None
        return ref[where] if rows is None else ref[where, rows, :]

    total = None
    for offset, factor in ((1, 8.0), (-1, -8.0), (2, -1.0), (-2, 1.0)):
        part = at(offset)
        if part is None:
            continue
        if total is None:
            total = factor * part if factor != 1.0 else part
        elif factor == -1.0:
            total = total - part
        elif factor == 1.0:
            total = total + part
        elif at(-offset) is not None and offset == -1:
            total = 8.0 * (at(1) - part)
        else:
            total = total + factor * part
    return total


def cross(left, right):
    return (
        left[1] * right[2] - left[2] * right[1],
        left[2] * right[0] - left[0] * right[2],
        left[0] * right[1] - left[1] * right[0],
    )


def split3(value):
    high = value.astype(jnp.bfloat16)
    rest = value - high.astype(F32)
    mid = rest.astype(jnp.bfloat16)
    return high, mid, (rest - mid.astype(F32)).astype(jnp.bfloat16)


def band():
    gap = lax.broadcasted_iota(jnp.int32, (LANES, LANES), 0) - lax.broadcasted_iota(jnp.int32, (LANES, LANES), 1)
    near = jnp.where(gap == 1, 8.0, jnp.where(gap == -1, -8.0, 0.0))
    far = jnp.where(gap == 2, -1.0, jnp.where(gap == -2, 1.0, 0.0))
    return (near + far).astype(jnp.bfloat16)


def edge_rows_matrix(block):
    row = lax.broadcasted_iota(jnp.int32, (16, LANES), 0) - 8 * (block % 2)
    col = lax.broadcasted_iota(jnp.int32, (16, LANES), 1)
    table = jnp.zeros((16, LANES), F32)
    for k, c, factor in ((2, 0, 1.0), (3, 0, -8.0), (3, 1, 1.0), (4, 126, -1.0), (4, 127, 8.0), (5, 127, -1.0)):
        table = jnp.where((row == k) & (col == c), factor, table)
    return table.astype(jnp.bfloat16)


def setup_body(mats):
    mats[...] = jnp.zeros(mats.shape, jnp.bfloat16)
    for block in range(mats.shape[0]):
        mats[block, :LANES, :] = band()
        start = LANES + 16 * (block // 2)
        mats[block, start : start + 16, :] = edge_rows_matrix(block)


def field_body(
    dirs, mats, m1, m2, w, d1, d2, xa, xb, e1x, e2x, ya, yb,
    g1_out, g2_out, h1_out, h2_out,
    g1, g2, h1, h2, out_sems,
    ext_refs, w_ext, s1, s2, hy1, hy2, hsrc1, hsrc2, cor1, cor2, ax, ay, az, lhs_f, lhs_a, res_f, res_a,
):
    core = lax.rem(lax.axis_index("gx"), 2)
    side = lax.rem(lax.axis_index("gy"), 2)
    full = (EXT, LANES)
    low = (lane(full) % 8) < 4
    flat = (LAYERS * EXT, LANES)
    flat16 = (LAYERS * ROWS, LANES)

    def put(lhs, index, value, right=False):
        rows = value.shape[0]
        for part, at in zip(split3(value), range(3)):
            start = (3 * index + at) * rows
            if right:
                lhs[start : start + rows, LANES:] = part
            else:
                lhs[start : start + rows, :LANES] = part

    def multiply(lhs, result, block):
        result[...] = jnp.dot(lhs[...], mats[block], preferred_element_type=F32)

    def column(result, rows, index, layer):
        per = result.shape[0] // 6
        start = 3 * index * per + layer * rows
        return (result[start : start + rows] + result[start + per : start + per + rows]) + result[
            start + 2 * per : start + 2 * per + rows
        ]

    def load_ext(slot, one, two, message):
        for layer in range(LAYERS):
            tail1, tail2 = join_rows(core, xa[message, layer], xb[message, layer])
            ext_refs[slot, 0, layer] = jnp.concatenate([one[layer], tail1], 0)
            ext_refs[slot, 1, layer] = jnp.concatenate([two[layer], tail2], 0)
        for index in (0, 1):
            put(lhs_f.at[slot], index, ext_refs[slot, index].reshape(flat))

    for layer in range(LAYERS):
        from_a, from_b = ya[layer], yb[layer]
        left = jnp.where(side == 0, from_b, from_a)
        right = jnp.where(side == 0, from_a, from_b)
        left2, right2 = lroll(left, -4), lroll(right, 4)
        for src, left_i, right_i, halo, hy in ((e1x, left, right, hsrc1, hy1), (e2x, left2, right2, hsrc2, hy2)):
            own = src[layer]
            before = diff_y(jnp.where(low, left_i, own))
            after = diff_y(jnp.where(low, own, right_i))
            halo[layer] = jnp.where(low, left_i, right_i)
            hy[layer] = jnp.where(low, before, after)
    for slot in (0, 1):
        for index, halo in ((0, hsrc1), (1, hsrc2)):
            put(lhs_f.at[slot], index, halo[...].reshape(flat), True)

    fold = -1.0 / 20736.0
    for layer in range(LAYERS):
        wt, _ = join_rows(core, xa[dirs + 1, layer], xb[dirs + 1, layer])
        w_ext[layer] = jnp.concatenate([w[layer], wt], 0) * fold

    def slopes(slot, index, layer):
        ext = ext_refs.at[slot, index]
        return diff_x(ext[layer]), column(res_f.at[slot], EXT, index, layer), diff_z(ext, layer)

    load_ext(0, m1, m2, dirs)
    multiply(lhs_f.at[0], res_f.at[0], dirs)
    multiply(lhs_f.at[0], res_f.at[1], dirs + 1)
    for layer in range(LAYERS):
        for index, ref in ((0, s1), (1, s2)):
            ext = ext_refs.at[0, index]
            ref[0, layer] = diff_x(ext[layer])
            ref[1, layer] = column(res_f.at[index], EXT, index, layer)
            ref[2, layer] = diff_z(ext, layer)

    main = pl.ds(0, ROWS)
    block = lane((ROWS, LANES)) // 8

    def spread(value, at):
        value = jnp.where(block == at, value, 0.0)
        for amount in (8, 16, 32, 64):
            value = value + lroll(value, amount)
        return value

    for layer in range(LAYERS):
        first = (diff_x(hsrc1[layer])[:ROWS], hy1[layer, main, :], diff_z(hsrc1, layer, main))
        second = (diff_x(hsrc2[layer])[:ROWS], hy2[layer, main, :], diff_z(hsrc2, layer, main))
        one = tuple(spread(part, dirs) for part in first)
        two = tuple(spread(part, dirs + 1) for part in second)
        weight = spread(hsrc1[layer, main, :], dirs + 1) * fold
        second = tuple(jnp.where(block == dirs, 0.0, part) for part in second)
        left_term = cross(first, two)
        right_term = cross(one, second)
        rw = tuple(weight * (left_term[i] + right_term[i]) for i in range(3))
        cor1[layer] = cross(two, rw)[1]
        cor2[layer] = cross(rw, one)[1]
    for slot in (0, 1):
        for index, cor in ((0, cor1), (1, cor2)):
            put(lhs_a.at[slot], index, cor[...].reshape(flat16), True)

    def products(slot, second_field):
        for layer in range(LAYERS):
            one = (s1[0, layer], s1[1, layer], s1[2, layer])
            two = (s2[0, layer], s2[1, layer], s2[2, layer])
            if second_field:
                perturbed = tuple(
                    p + q for p, q in zip(cross(slopes(slot, 0, layer), two), cross(one, slopes(slot, 1, layer)))
                )
            else:
                perturbed = cross(one, two)
            weight = w_ext[layer]
            rw = tuple(weight * part for part in perturbed)
            for k, adj in ((0, cross(two, rw)), (1, cross(rw, one))):
                ax[slot, k, layer] = adj[0]
                ay[slot, k, layer] = adj[1][:ROWS]
                az[slot, k, layer] = adj[2][:ROWS]
        for k in (0, 1):
            put(lhs_a.at[slot], k, ay[slot, k].reshape(flat16))

    def divergence(slot, outs):
        for k in (0, 1):
            for layer in range(LAYERS):
                outs[k][layer] = (
                    diff_x(ax[slot, k, layer])[:ROWS]
                    + column(res_a.at[slot], ROWS, k, layer)
                    + diff_z(az.at[slot, k], layer)
                )

    def results(d):
        return (
            pltpu.make_async_copy(h1.at[d], h1_out.at[d], out_sems.at[0, d]),
            pltpu.make_async_copy(h2.at[d], h2_out.at[d], out_sems.at[1, d]),
        )

    products(0, False)
    multiply(lhs_a.at[0], res_a.at[0], dirs)
    divergence(0, (g1, g2))
    last = (
        pltpu.make_async_copy(g1, g1_out, out_sems.at[0, dirs]),
        pltpu.make_async_copy(g2, g2_out, out_sems.at[1, dirs]),
    )
    for copy in last:
        copy.start()

    @pl.loop(0, dirs // 2)
    def _(step):
        d, e = 2 * step, 2 * step + 1
        load_ext(0, d1.at[d], d2.at[d], d)
        multiply(lhs_f.at[0], res_f.at[0], d)
        load_ext(1, d1.at[e], d2.at[e], e)
        multiply(lhs_f.at[1], res_f.at[1], e)
        products(0, True)
        multiply(lhs_a.at[0], res_a.at[0], d)
        products(1, True)
        multiply(lhs_a.at[1], res_a.at[1], e)
        divergence(0, (h1.at[d], h2.at[d]))
        divergence(1, (h1.at[e], h2.at[e]))
        for at in (d, e):
            for copy in results(at):
                copy.start()

    @pl.loop(0, dirs)
    def _(d):
        for copy in results(d):
            copy.wait()

    for copy in last:
        copy.wait()


def params():
    return pltpu.CompilerParams(vmem_limit_bytes=40 * MIB)


def shards(model_one, model_two, weight, direction_one, direction_two):
    dirs = direction_one.shape[0]
    tile = shape(LAYERS, ROWS, LANES)
    ext = shape(LAYERS, EXT, LANES)
    small = shape(LAYERS, 8, LANES)
    fields = (model_one, model_two, weight, direction_one, direction_two)
    mats = pl.pallas_call(
        setup_body,
        out_shape=jax.ShapeDtypeStruct((dirs + 2, 2 * LANES, LANES), jnp.bfloat16),
        cost_estimate=pl.CostEstimate(flops=0, bytes_accessed=8 * MIB, transcendentals=0),
        compiler_params=params(),
        name="setup",
    )()
    any_spec = pl.BlockSpec(memory_space=pl.ANY)
    vmem_spec = pl.BlockSpec(memory_space=pltpu.VMEM)
    xs, xa, e1, e2 = pl.pallas_call(
        functools.partial(pack_body, dirs),
        out_shape=(small, shape(dirs + 3, LAYERS, 8, LANES), tile, tile),
        in_specs=[any_spec] + [vmem_spec] * 5,
        compiler_params=params(),
        name="pack",
    )(mats, *fields)
    count_x, count_y = lax.axis_size("gx"), lax.axis_size("gy")
    xs = lax.ppermute(xs, "gx", swap(count_x, 1))
    xa = lax.ppermute(xa, "gx", swap(count_x, 0))
    xb = pl.pallas_call(
        functools.partial(far_body, dirs),
        out_shape=shape(dirs + 2, LAYERS, 8, LANES),
        in_specs=[any_spec] + [vmem_spec] * 5,
        compiler_params=params(),
        name="far",
    )(xs, *fields)
    xb = lax.ppermute(xb, "gx", swap(count_x, 1))
    e1x, e2x, ya, yb = pl.pallas_call(
        edges_body,
        out_shape=(ext,) * 4,
        compiler_params=params(),
        name="edges",
    )(e1, e2, xa[dirs + 2], xs)
    yb = lax.ppermute(yb, "gy", swap(count_y, 1))
    ya = lax.ppermute(ya, "gy", swap(count_y, 0))
    many = shape(dirs, LAYERS, ROWS, LANES)
    ext_s = scratch(LAYERS, EXT, LANES)
    ext_3 = scratch(3, LAYERS, EXT, LANES)
    tile_s = scratch(LAYERS, ROWS, LANES)
    pair_s = scratch(2, 2, LAYERS, ROWS, LANES)
    many_s = scratch(dirs, LAYERS, ROWS, LANES)
    return pl.pallas_call(
        functools.partial(field_body, dirs),
        out_shape=(tile, tile, many, many),
        out_specs=[pl.BlockSpec(memory_space=pltpu.HBM)] * 4,
        scratch_shapes=[
            tile_s, tile_s, many_s, many_s, pltpu.SemaphoreType.DMA((2, dirs + 1)),
            scratch(2, 2, LAYERS, EXT, LANES), ext_s, ext_3, ext_3, ext_s, ext_s, ext_s, ext_s, tile_s, tile_s,
            scratch(2, 2, LAYERS, EXT, LANES), pair_s, pair_s,
            half(2, 6 * LAYERS * EXT, 2 * LANES), half(2, 6 * LAYERS * ROWS, 2 * LANES),
            scratch(2, 6 * LAYERS * EXT, LANES), scratch(2, 6 * LAYERS * ROWS, LANES),
        ],
        compiler_params=params(),
        name="fields",
    )(mats, *fields, xa, xb, e1x, e2x, ya, yb)


def solution(mesh):
    plane = P(None, "gx", "gy")
    stack = P(None, None, "gx", "gy")
    return jax.shard_map(
        shards,
        mesh=mesh,
        in_specs=(plane, plane, plane, stack, stack),
        out_specs=(plane, plane, stack, stack),
        check_vma=False,
    )
```

time: 50.5 us -> 36.8 us (0.73)
  Pallas kernels: 20.2 us -> 8.48 us
  starting transfers between devices: 17 us -> 19.2 us
  waiting for transfers between devices: 7.45 us -> 5.27 us
  local copies, waits for them, and re-layouts: 4.7 us -> 2.87 us
    pallas_call x1, Pallas kernels: 19.4 us -> 7.68 us  [shards(): pl.pallas_call(functools.partial(field_body, dirs), out_shape=(tile, tile...]
    ppermute x1, starting transfers between devices: 2.74 us -> 4.94 us  [shards(): xs = lax.ppermute(xs, 'gx', swap(count_x, 1))]
    ppermute x1, waiting for transfers between devices: 4.58 us -> 2.4 us  [shards(): xs = lax.ppermute(xs, 'gx', swap(count_x, 1))]
    unnamed x18 -> x14, local copies, waits for them, and re-layouts: 4.7 us -> 2.86 us
where the time goes in v2:
time: 36.8 us; the launch traced here: 36.6 us
  starting transfers between devices  19.2 us (52%)
  Pallas kernels  8.48 us (23%)
  waiting for transfers between devices  5.27 us (14%)
  local copies, waits for them, and re-layouts  2.87 us (8%)
  between operations  0.75 us (2%)
    pallas_call x1, Pallas kernels, shards(): pl.pallas_call(functools.partial(field_body, dirs), out_shape=(tile, tile...  7.68 us
    ppermute x1, starting transfers between devices, shards(): yb = lax.ppermute(yb, 'gy', swap(count_y, 1))  7.22 us
    ppermute x1, starting transfers between devices, shards(): xs = lax.ppermute(xs, 'gx', swap(count_x, 1))  4.94 us
    ppermute x1, starting transfers between devices, shards(): xb = lax.ppermute(xb, 'gx', swap(count_x, 1))  4.94 us
    unnamed x14, local copies, waits for them, and re-layouts  2.86 us
    ppermute x1, waiting for transfers between devices, shards(): yb = lax.ppermute(yb, 'gy', swap(count_y, 1))  2.86 us
    ppermute x1, waiting for transfers between devices, shards(): xs = lax.ppermute(xs, 'gx', swap(count_x, 1))  2.4 us
    ppermute x1, starting transfers between devices, shards(): ya = lax.ppermute(ya, 'gy', swap(count_y, 0))  2 us
  transfers between devices with their start and end apart: 5, of which 2 were waited for; matrix products, arithmetic and copies ran while one was open for 0% of the time, Pallas kernels for 0%

profile of v2, /device:TPU:24, one launch (start us, length us, event | category | flops | bytes accessed | tf_op | source)
XLA Modules:
  0.0 36.6 jit_solution(1327180445382435597)
XLA Ops:
  0.6 0.0 copy-start
  0.6 0.0 copy-start.4
  0.7 0.0 copy-start.3
  0.7 0.1 setup.1.first.mats
  0.8 0.9 %copy-done = f32[10,8,16,128]{3,2,1,0:T(8,128)S(1)} copy-done((f32[10,8,16,128]{3,2,1,0:T(8,128)S(1)}, f32[10,8,16,128]{3,2,1,0:T(8,128)}, u32[]{:S(2)}) %copy-start) | copy-done | bytes 655384
  1.7 0.0 copy-done.4
  1.7 0.0 copy-done.3
  1.7 0.0 copy-start.1
  1.7 1.1 %copy-done.1 = f32[10,8,16,128]{3,2,1,0:T(8,128)S(1)} copy-done((f32[10,8,16,128]{3,2,1,0:T(8,128)S(1)}, f32[10,8,16,128]{3,2,1,0:T(8,128)}, u32[]{:S(2)}) %copy-start.1) | copy-done | bytes 655384
  2.8 0.0 copy-start.5
  2.8 0.8 %copy-done.5 = f32[8,16,128]{2,1,0:T(8,128)S(1)} copy-done((f32[8,16,128]{2,1,0:T(8,128)S(1)}, f32[8,16,128]{2,1,0:T(8,128)}, u32[]{:S(2)}) %copy-start.5) | copy-done | bytes 65560
  3.7 0.0 copy-start.2
  3.7 0.5 %pack.1 = (f32[8,8,128]{2,1,0:T(8,128)S(1)}, f32[13,8,8,128]{3,2,1,0:T(8,128)S(1)}, f32[8,16,128]{2,1,0:T(8,128)S(1)}, f32[8,16,128]{2,1,0:T(8,128)S(1)}) custom-call(bf16[12,256,128]{2,1,0:T(8,128)(2,1)S(1)} %setup.1.first.mats, f32[8,16,128]{2,1,0:T(8,128)S(1)} %copy-done.3, f32[8,16,128]{2,1,0:T(8,128)S(1)} %copy-done.4, f32[8,16,128]{2,1,0:T(8,128)S(1)} %copy-done.5, ...), custom_call_target="tpu_custom_call" | custom-call | tf_op jit(solution)/shard_map/pack/pallas_call | solution.py:385
  4.1 0.1 collective-permute-start
  4.2 4.9 %collective-permute-start.1 = (f32[8,8,128]{2,1,0:T(8,128)S(1)}, f32[8,8,128]{2,1,0:T(8,128)S(1)}, u32[]{:S(2)}, u32[]{:S(2)}) collective-permute-start(f32[8,8,128]{2,1,0:T(8,128)S(1)} %get-tuple-element.13), channel_id=1, source_target_pairs={{16,32},{32,16},{48,64},{64,48},{80,96},{96,80},{112,128},{128,112... | collective-permute-start | bytes 98312 | tf_op jit(solution)/shard_map/ppermute | solution.py:393
  9.2 2.4 %collective-permute-done.1.first.xs = f32[8,8,128]{2,1,0:T(8,128)S(1)} collective-permute-done((f32[8,8,128]{2,1,0:T(8,128)S(1)}, f32[8,8,128]{2,1,0:T(8,128)S(1)}, u32[]{:S(2)}, u32[]{:S(2)}) %collective-permute-start.1) | collective-permute-done | bytes 32800 | tf_op jit(solution)/shard_map/ppermute | solution.py:393
  11.6 0.0 copy-done.2
  11.6 0.1 far.1
  11.7 4.9 %collective-permute-start.2 = (f32[12,8,8,128]{3,2,1,0:T(8,128)S(1)}, f32[12,8,8,128]{3,2,1,0:T(8,128)S(1)}, u32[]{:S(2)}, u32[]{:S(2)}) collective-permute-start(f32[12,8,8,128]{3,2,1,0:T(8,128)S(1)} %far.1), channel_id=1, source_target_pairs={{16,32},{32,16},{48,64},{64,48},{80,96},{96,80},{112,128},{128,112... | collective-permute-start | bytes 1179656 | tf_op jit(solution)/shard_map/ppermute | solution.py:402
  16.6 0.0 collective-permute-done.xa
  16.6 0.0 copy-start.6
  16.6 0.1 edges.1
  16.8 2.0 %collective-permute-start.3 = (f32[8,24,128]{2,1,0:T(8,128)S(1)}, f32[8,24,128]{2,1,0:T(8,128)S(1)}, u32[]{:S(2)}, u32[]{:S(2)}) collective-permute-start(f32[8,24,128]{2,1,0:T(8,128)S(1)} %get-tuple-element.18), channel_id=1, source_target_pairs={{0,1},{1,0},{2,3},{3,2},{4,5},{5,4},{6,7},{7,6},{8,9},{9,8},{10,11... | collective-permute-start | bytes 294920 | tf_op jit(solution)/shard_map/ppermute | solution.py:410
  18.8 7.2 %collective-permute-start.4 = (f32[8,24,128]{2,1,0:T(8,128)S(1)}, f32[8,24,128]{2,1,0:T(8,128)S(1)}, u32[]{:S(2)}, u32[]{:S(2)}) collective-permute-start(f32[8,24,128]{2,1,0:T(8,128)S(1)} %get-tuple-element.19), channel_id=1, source_target_pairs={{1,2},{2,1},{3,4},{4,3},{5,6},{6,5},{7,8},{8,7},{9,10},{10,9},{11,... | collective-permute-start | bytes 294920 | tf_op jit(solution)/shard_map/ppermute | solution.py:409
  26.0 0.0 collective-permute-done.2.xb
  26.0 0.0 collective-permute-done.3.ya
  26.0 2.9 %collective-permute-done.4.yb = f32[8,24,128]{2,1,0:T(8,128)S(1)} collective-permute-done((f32[8,24,128]{2,1,0:T(8,128)S(1)}, f32[8,24,128]{2,1,0:T(8,128)S(1)}, u32[]{:S(2)}, u32[]{:S(2)}) %collective-permute-start.4) | collective-permute-done | bytes 98336 | tf_op jit(solution)/shard_map/ppermute | solution.py:409
  28.9 0.0 copy-done.6
  28.9 7.7 %fields.1 = (f32[8,16,128]{2,1,0:T(8,128)}, f32[8,16,128]{2,1,0:T(8,128)}, f32[10,8,16,128]{3,2,1,0:T(8,128)}, f32[10,8,16,128]{3,2,1,0:T(8,128)}) custom-call(bf16[12,256,128]{2,1,0:T(8,128)(2,1)S(1)} %setup.1.first.mats, f32[8,16,128]{2,1,0:T(8,128)S(1)} %copy-done.3, f32[8,16,128]{2,1,0:T(8,128)S(1)} %copy-done.4, f32[8,16,128]{2,1,0:T(8,128)S(1)} %copy-done.6, ...), custom_call_target="tpu_custom_call" | custom-call | tf_op jit(solution)/shard_map/fields/pallas_call | solution.py:417
  (1 shorter events, 0.0 us)
Async XLA Ops:
  0.6 1.1 %copy-start = (f32[10,8,16,128]{3,2,1,0:T(8,128)S(1)}, f32[10,8,16,128]{3,2,1,0:T(8,128)}, u32[]{:S(2)}) copy-start(f32[10,8,16,128]{3,2,1,0:T(8,128)} %d1.5) | copy-start | bytes 1966084
  0.6 1.1 %copy-start.4 = (f32[8,16,128]{2,1,0:T(8,128)S(1)}, f32[8,16,128]{2,1,0:T(8,128)}, u32[]{:S(2)}) copy-start(f32[8,16,128]{2,1,0:T(8,128)} %m2.5) | copy-start | bytes 196612
  0.7 1.1 %copy-start.3 = (f32[8,16,128]{2,1,0:T(8,128)S(1)}, f32[8,16,128]{2,1,0:T(8,128)}, u32[]{:S(2)}) copy-start(f32[8,16,128]{2,1,0:T(8,128)} %m1.5) | copy-start | bytes 196612
  1.7 1.1 %copy-start.1 = (f32[10,8,16,128]{3,2,1,0:T(8,128)S(1)}, f32[10,8,16,128]{3,2,1,0:T(8,128)}, u32[]{:S(2)}) copy-start(f32[10,8,16,128]{3,2,1,0:T(8,128)} %d2.5) | copy-start | bytes 1966084
  2.8 0.8 %copy-start.5 = (f32[8,16,128]{2,1,0:T(8,128)S(1)}, f32[8,16,128]{2,1,0:T(8,128)}, u32[]{:S(2)}) copy-start(f32[8,16,128]{2,1,0:T(8,128)} %w.5) | copy-start | bytes 196612
  3.7 7.9 %copy-start.2 = (f32[10,8,16,128]{3,2,1,0:T(8,128)S(1)}, f32[10,8,16,128]{3,2,1,0:T(8,128)}, u32[]{:S(2)}) copy-start(f32[10,8,16,128]{3,2,1,0:T(8,128)} %d2.5) | copy-start | bytes 1966084
  4.1 12.5 %collective-permute-start = (f32[13,8,8,128]{3,2,1,0:T(8,128)S(1)}, f32[13,8,8,128]{3,2,1,0:T(8,128)S(1)}, u32[]{:S(2)}, u32[]{:S(2)}) collective-permute-start(f32[13,8,8,128]{3,2,1,0:T(8,128)S(1)} %get-tuple-element.12), channel_id=1, source_target_pairs={{0,16},{16,0},{32,48},{48,32},{64,80},{80,64},{96,112},{112,96},{1... | collective-permute-start | bytes 1277960 | tf_op jit(solution)/shard_map/ppermute | solution.py:394
  4.2 7.3 %collective-permute-start.1 = (f32[8,8,128]{2,1,0:T(8,128)S(1)}, f32[8,8,128]{2,1,0:T(8,128)S(1)}, u32[]{:S(2)}, u32[]{:S(2)}) collective-permute-start(f32[8,8,128]{2,1,0:T(8,128)S(1)} %get-tuple-element.13), channel_id=1, source_target_pairs={{16,32},{32,16},{48,64},{64,48},{80,96},{96,80},{112,128},{128,112... | collective-permute-start | bytes 98312 | tf_op jit(solution)/shard_map/ppermute | solution.py:393
  11.7 14.3 %collective-permute-start.2 = (f32[12,8,8,128]{3,2,1,0:T(8,128)S(1)}, f32[12,8,8,128]{3,2,1,0:T(8,128)S(1)}, u32[]{:S(2)}, u32[]{:S(2)}) collective-permute-start(f32[12,8,8,128]{3,2,1,0:T(8,128)S(1)} %far.1), channel_id=1, source_target_pairs={{16,32},{32,16},{48,64},{64,48},{80,96},{96,80},{112,128},{128,112... | collective-permute-start | bytes 1179656 | tf_op jit(solution)/shard_map/ppermute | solution.py:402
  16.6 12.3 %copy-start.6 = (f32[8,16,128]{2,1,0:T(8,128)S(1)}, f32[8,16,128]{2,1,0:T(8,128)}, u32[]{:S(2)}) copy-start(f32[8,16,128]{2,1,0:T(8,128)} %w.5) | copy-start | bytes 196612
  16.8 9.2 %collective-permute-start.3 = (f32[8,24,128]{2,1,0:T(8,128)S(1)}, f32[8,24,128]{2,1,0:T(8,128)S(1)}, u32[]{:S(2)}, u32[]{:S(2)}) collective-permute-start(f32[8,24,128]{2,1,0:T(8,128)S(1)} %get-tuple-element.18), channel_id=1, source_target_pairs={{0,1},{1,0},{2,3},{3,2},{4,5},{5,4},{6,7},{7,6},{8,9},{9,8},{10,11... | collective-permute-start | bytes 294920 | tf_op jit(solution)/shard_map/ppermute | solution.py:410
  18.8 10.1 %collective-permute-start.4 = (f32[8,24,128]{2,1,0:T(8,128)S(1)}, f32[8,24,128]{2,1,0:T(8,128)S(1)}, u32[]{:S(2)}, u32[]{:S(2)}) collective-permute-start(f32[8,24,128]{2,1,0:T(8,128)S(1)} %get-tuple-element.19), channel_id=1, source_target_pairs={{1,2},{2,1},{3,4},{4,3},{5,6},{6,5},{7,8},{8,7},{9,10},{10,9},{11,... | collective-permute-start | bytes 294920 | tf_op jit(solution)/shard_map/ppermute | solution.py:409

commit v3 on v2

v3 whole, which is shorter than its diff:
```python
import functools

import jax
import jax.numpy as jnp
from jax import lax
from jax.experimental import pallas as pl
from jax.experimental.pallas import tpu as pltpu
from jax.sharding import PartitionSpec as P

LAYERS = 8
ROWS = 16
EXT = 32
LANES = 128
MIB = 1024 * 1024
F32 = jnp.float32


def swap(count, first):
    pairs = []
    for low in range(first, count - 1, 2):
        pairs += [(low, low + 1), (low + 1, low)]
    return pairs


def shape(*dims):
    return jax.ShapeDtypeStruct(dims, F32)


def scratch(*dims):
    return pltpu.VMEM(dims, F32)


def half(*dims):
    return pltpu.VMEM(dims, jnp.bfloat16)


def lane(dims):
    return lax.broadcasted_iota(jnp.int32, dims, len(dims) - 1)


def sub(dims):
    return lax.broadcasted_iota(jnp.int32, dims, len(dims) - 2)


def lroll(value, amount):
    return pltpu.roll(value, amount % LANES, axis=value.ndim - 1)


def sroll(value, amount):
    return pltpu.roll(value, amount % value.shape[-2], axis=value.ndim - 2)


def pack_body(dirs, first, m1, m2, w, d1, d2, e1, e2, ya, yb):
    side = lax.rem(lax.axis_index("gy"), 2)
    block = lane((ROWS, LANES)) // 8
    low = (lane((ROWS, LANES)) % 8) < 4
    for layer in range(LAYERS):
        one = jnp.zeros((ROWS, LANES), F32)
        two = jnp.zeros((ROWS, LANES), F32)
        for d in range(dirs):
            one = jnp.where(block == d, lroll(d1[d, layer], 8 * d + 4), one)
            two = jnp.where(block == d, lroll(d2[d, layer], 8 * d + 4), two)
        one = jnp.where(block == dirs, lroll(m1[layer], 8 * dirs + 4), one)
        one = jnp.where(block == dirs + 1, lroll(w[layer], 8 * dirs + 12), one)
        two = jnp.where(block == dirs + 1, lroll(m2[layer], 8 * dirs + 12), two)
        e1[layer] = one
        e2[layer] = two
        tail = jnp.where(low, one, lroll(two, 4))
        head = jnp.where(low, lroll(two, -4), one)
        ya[layer] = jnp.where(side == 0, tail, head)
        yb[layer] = jnp.where(side == 0, head, tail)


def edge_rows(one, two, tail, layer):
    upper = (sub((8, LANES)) >= 4).astype(jnp.int32)
    start = pl.multiple_of(tail * 8, 8)
    first = one[layer, pl.ds(start, 8), :]
    second = two[layer, pl.ds(start, 8), :]
    return jnp.where(upper == tail, first, sroll(second, 4))


def sides(ya, yb, layer):
    side = lax.rem(lax.axis_index("gy"), 2)
    from_a, from_b = ya[layer], yb[layer]
    left = jnp.where(side == 0, from_b, from_a)
    right = jnp.where(side == 0, from_a, from_b)
    return left, right, lroll(left, -4), lroll(right, 4)


def rows_body(dirs, ya, yb, m1, m2, w, d1, d2, xa, xb, hm):
    core = lax.rem(lax.axis_index("gx"), 2)
    low = (lane((ROWS, LANES)) % 8) < 4
    for layer in range(LAYERS):
        left, right, left2, right2 = sides(ya, yb, layer)
        hm[0, layer] = jnp.where(low, left, right)
        hm[1, layer] = jnp.where(low, left2, right2)
    pairs = [(d1.at[d], d2.at[d]) for d in range(dirs)] + [(m1, m2), (w, w), (hm.at[0], hm.at[1])]
    for index, (one, two) in enumerate(pairs):
        for layer in range(LAYERS):
            xa[index, layer] = edge_rows(one, two, 1 - core, layer)
            xb[index, layer] = edge_rows(one, two, core, layer)


def stencil(up2, up1, down1, down2):
    return 8.0 * (up1 - down1) - (up2 - down2)


def diff_x(ref, layer, start, rows):
    at = lambda offset: ref[layer, pl.ds(start + offset, rows), :]
    return stencil(at(2), at(1), at(-1), at(-2))


def diff_y(value):
    return stencil(lroll(value, -2), lroll(value, -1), lroll(value, 1), lroll(value, 2))


def diff_z(ref, layer, start, rows):
    def at(offset):
        where = layer + offset
        return ref[where, pl.ds(start, rows), :] if 0 <= where < LAYERS else None

    up2, up1, down1, down2 = at(2), at(1), at(-1), at(-2)
    if up1 is None:
        total = -8.0 * down1
    elif down1 is None:
        total = 8.0 * up1
    else:
        total = 8.0 * (up1 - down1)
    if up2 is not None:
        total = total - up2
    if down2 is not None:
        total = total + down2
    return total


def cross(left, right):
    return (
        left[1] * right[2] - left[2] * right[1],
        left[2] * right[0] - left[0] * right[2],
        left[0] * right[1] - left[1] * right[0],
    )


def split3(value):
    high = value.astype(jnp.bfloat16)
    rest = value - high.astype(F32)
    mid = rest.astype(jnp.bfloat16)
    return high, mid, (rest - mid.astype(F32)).astype(jnp.bfloat16)


def band():
    gap = lax.broadcasted_iota(jnp.int32, (LANES, LANES), 0) - lax.broadcasted_iota(jnp.int32, (LANES, LANES), 1)
    near = jnp.where(gap == 1, 8.0, jnp.where(gap == -1, -8.0, 0.0))
    far = jnp.where(gap == 2, -1.0, jnp.where(gap == -2, 1.0, 0.0))
    return (near + far).astype(jnp.bfloat16)


def edge_rows_matrix(block):
    row = lax.broadcasted_iota(jnp.int32, (16, LANES), 0) - 8 * (block % 2)
    col = lax.broadcasted_iota(jnp.int32, (16, LANES), 1)
    table = jnp.zeros((16, LANES), F32)
    for k, c, factor in ((2, 0, 1.0), (3, 0, -8.0), (3, 1, 1.0), (4, 126, -1.0), (4, 127, 8.0), (5, 127, -1.0)):
        table = jnp.where((row == k) & (col == c), factor, table)
    return table.astype(jnp.bfloat16)


def setup_body(mats):
    mats[...] = jnp.zeros(mats.shape, jnp.bfloat16)
    for block in range(mats.shape[0]):
        mats[block, :LANES, :] = band()
        start = LANES + 16 * (block // 2)
        mats[block, start : start + 16, :] = edge_rows_matrix(block)


def phase(dirs, rows, wide, first_row, mats, m1, m2, w, d1, d2, message, hm, hy, outs, done, refs):
    ext_refs, h_ext, w_ext, s1, s2, cor, ax, ay, az, lhs_f, lhs_a, res_f, res_a = refs
    start = first_row + 8
    flat = (LAYERS * rows, LANES)
    flat_out = (LAYERS * wide, LANES)
    main = pl.ds(start, rows)

    def put(lhs, index, value, right=False):
        count = value.shape[0]
        for at, part in enumerate(split3(value)):
            begin = (3 * index + at) * count
            if right:
                lhs[begin : begin + count, LANES:] = part
            else:
                lhs[begin : begin + count, :LANES] = part

    def multiply(lhs, result, block, index=None):
        each = lhs.shape[0] // 2
        span = slice(0, 2 * each) if index is None else slice(index * each, (index + 1) * each)
        result[span] = jnp.dot(lhs[span], mats[block], preferred_element_type=F32)

    def column(result, index, layer):
        per = result.shape[0] // 6
        count = per // LAYERS
        begin = 3 * index * per + layer * count
        part = lambda at: result[begin + at * per : begin + at * per + count]
        return (part(0) + part(1)) + part(2)

    def fill(ext, own, beside, layer):
        ext[layer, 0:8, :] = beside
        ext[layer, 8:24, :] = own[layer]
        ext[layer, 24:32, :] = beside

    def load_ext(slot, one, two, index):
        for layer in range(LAYERS):
            beside = message[index, layer]
            fill(ext_refs.at[slot, 0], one, beside, layer)
            fill(ext_refs.at[slot, 1], two, sroll(beside, 4), layer)
        for k in (0, 1):
            put(lhs_f.at[slot], k, ext_refs[slot, k, :, main, :].reshape(flat))

    for layer in range(LAYERS):
        beside = message[dirs + 2, layer]
        fill(h_ext.at[0], hm.at[0], beside, layer)
        fill(h_ext.at[1], hm.at[1], sroll(beside, 4), layer)
        fill(w_ext, w, message[dirs + 1, layer], layer)
    for k in (0, 1):
        put(lhs_f.at[0], k, h_ext[k, :, main, :].reshape(flat), True)
    load_ext(0, m1, m2, dirs)
    multiply(lhs_f.at[0], res_f.at[0], dirs, 0)
    multiply(lhs_f.at[0], res_f.at[0], dirs + 1, 1)
    for k in (0, 1):
        put(lhs_f.at[1], k, h_ext[k, :, main, :].reshape(flat), True)

    def slopes(slot, k, layer):
        ext = ext_refs.at[slot, k]
        return (
            diff_x(ext, layer, start, rows),
            column(res_f.at[slot], k, layer),
            diff_z(ext, layer, start, rows),
        )

    fold = -1.0 / 20736.0
    block = lane((rows, LANES)) // 8
    within = lane((rows, LANES)) % 8

    def spread(value, at):
        return jnp.take_along_axis(value, within + 8 * at, axis=1)

    for layer in range(LAYERS):
        first, second = (
            (
                diff_x(h_ext.at[k], layer, start, rows),
                hy[k, layer, main, :],
                diff_z(h_ext.at[k], layer, start, rows),
            )
            for k in (0, 1)
        )
        one = tuple(spread(part, dirs) for part in first)
        two = tuple(spread(part, dirs + 1) for part in second)
        weight = spread(h_ext[0, layer, main, :], dirs + 1) * fold
        second = tuple(jnp.where(block == dirs, 0.0, part) for part in second)
        left_term = cross(first, two)
        right_term = cross(one, second)
        rw = tuple(weight * (left_term[i] + right_term[i]) for i in range(3))
        cor[0, layer, :rows, :] = cross(two, rw)[1]
        cor[1, layer, :rows, :] = cross(rw, one)[1]
    for slot in (0, 1):
        for k in (0, 1):
            put(lhs_a.at[slot], k, cor[k, :, 2 : 2 + wide, :].reshape(flat_out), True)

    for layer in range(LAYERS):
        for k, ref in ((0, s1), (1, s2)):
            for index, part in enumerate(slopes(0, k, layer)):
                ref[index, layer] = part

    def products(slot, second_field):
        for layer in range(LAYERS):
            one = (s1[0, layer], s1[1, layer], s1[2, layer])
            two = (s2[0, layer], s2[1, layer], s2[2, layer])
            if second_field:
                perturbed = tuple(
                    p + q for p, q in zip(cross(slopes(slot, 0, layer), two), cross(one, slopes(slot, 1, layer)))
                )
            else:
                perturbed = cross(one, two)
            weight = w_ext[layer, main, :] * fold
            rw = tuple(weight * part for part in perturbed)
            for k, adj in ((0, cross(two, rw)), (1, cross(rw, one))):
                ax[slot, k, layer, :rows, :] = adj[0]
                ay[slot, k, layer, :rows, :] = adj[1]
                az[slot, k, layer, :rows, :] = adj[2]
        for k in (0, 1):
            put(lhs_a.at[slot], k, ay[slot, k, :, 2 : 2 + wide, :].reshape(flat_out))

    def divergence(slot, targets):
        for k in (0, 1):
            for layer in range(LAYERS):
                total = (
                    diff_x(ax.at[slot, k], layer, 2, wide)
                    + column(res_a.at[slot], k, layer)
                    + diff_z(az.at[slot, k], layer, 2, wide)
                )
                targets[k][layer, pl.ds(first_row + 2, rows - 4), :] = total[: rows - 4]

    g1, g2, h1, h2 = outs
    products(0, False)
    multiply(lhs_a.at[0], res_a.at[0], dirs)
    divergence(0, (g1, g2))
    done(None)

    @pl.loop(0, dirs // 2)
    def _(step):
        d, e = 2 * step, 2 * step + 1
        load_ext(0, d1.at[d], d2.at[d], d)
        multiply(lhs_f.at[0], res_f.at[0], d)
        load_ext(1, d1.at[e], d2.at[e], e)
        multiply(lhs_f.at[1], res_f.at[1], e)
        products(0, True)
        multiply(lhs_a.at[0], res_a.at[0], d)
        products(1, True)
        multiply(lhs_a.at[1], res_a.at[1], e)
        divergence(0, (h1.at[d], h2.at[d]))
        divergence(1, (h1.at[e], h2.at[e]))
        done(d)
        done(e)


def phase_scratch(rows, wide):
    ext = scratch(LAYERS, EXT, LANES)
    slopes = scratch(3, LAYERS, rows, LANES)
    adjoint = scratch(2, 2, LAYERS, rows + 16, LANES)
    return [
        scratch(2, 2, LAYERS, EXT, LANES), scratch(2, LAYERS, EXT, LANES), ext, slopes, slopes,
        scratch(2, LAYERS, rows + 16, LANES), adjoint, adjoint, adjoint,
        half(2, 6 * LAYERS * rows, 2 * LANES), half(2, 6 * LAYERS * wide, 2 * LANES),
        scratch(2, 6 * LAYERS * rows, LANES), scratch(2, 6 * LAYERS * wide, LANES),
    ]


def near_body(dirs, mats, m1, m2, w, d1, d2, xa, hm, e1, e2, ya, yb, g1, g2, h1, h2, hy, *refs):
    core = lax.rem(lax.axis_index("gx"), 2)
    low = (lane((ROWS, LANES)) % 8) < 4
    for layer in range(LAYERS):
        left, right, left2, right2 = sides(ya, yb, layer)
        for k, own, before, after in ((0, e1[layer], left, right), (1, e2[layer], left2, right2)):
            before = diff_y(jnp.where(low, before, own))
            after = diff_y(jnp.where(low, own, after))
            hy[k, layer, 8:24, :] = jnp.where(low, before, after)
            hy[k, layer, 0:8, :] = jnp.zeros((8, LANES), F32)
            hy[k, layer, 24:32, :] = jnp.zeros((8, LANES), F32)
    phase(
        dirs, 16, 16, 2 - 4 * core, mats, m1, m2, w, d1, d2, xa, hm, hy, (g1, g2, h1, h2), lambda d: None, refs
    )


def rest_body(
    dirs, mats, m1, m2, w, d1, d2, xb, hm, hy, g1_in, g2_in, h1_in, h2_in,
    g1_out, g2_out, h1_out, h2_out, g1, g2, h1, h2, sems, *refs,
):
    core = lax.rem(lax.axis_index("gx"), 2)

    def copies(d):
        if d is None:
            return (
                pltpu.make_async_copy(g1, g1_out, sems.at[0, dirs]),
                pltpu.make_async_copy(g2, g2_out, sems.at[1, dirs]),
            )
        return (
            pltpu.make_async_copy(h1.at[d], h1_out.at[d], sems.at[0, d]),
            pltpu.make_async_copy(h2.at[d], h2_out.at[d], sems.at[1, d]),
        )

    def done(d):
        for copy in copies(d):
            copy.start()

    g1[...] = g1_in[...]
    g2[...] = g2_in[...]
    h1[...] = h1_in[...]
    h2[...] = h2_in[...]
    phase(dirs, 8, 8, 12 * core - 2, mats, m1, m2, w, d1, d2, xb, hm, hy, (g1, g2, h1, h2), done, refs)

    @pl.loop(0, dirs)
    def _(d):
        for copy in copies(d):
            copy.wait()

    for copy in copies(None):
        copy.wait()


def params():
    return pltpu.CompilerParams(vmem_limit_bytes=40 * MIB)


def cost(mib):
    return pl.CostEstimate(flops=0, bytes_accessed=mib * MIB, transcendentals=0)


def shards(model_one, model_two, weight, direction_one, direction_two):
    dirs = direction_one.shape[0]
    tile = shape(LAYERS, ROWS, LANES)
    many = shape(dirs, LAYERS, ROWS, LANES)
    message = shape(dirs + 3, LAYERS, 8, LANES)
    tile_s = scratch(LAYERS, ROWS, LANES)
    many_s = scratch(dirs, LAYERS, ROWS, LANES)
    fields = (model_one, model_two, weight, direction_one, direction_two)
    count_x, count_y = lax.axis_size("gx"), lax.axis_size("gy")
    any_spec = pl.BlockSpec(memory_space=pl.ANY)
    vmem_spec = pl.BlockSpec(memory_space=pltpu.VMEM)
    mats = pl.pallas_call(
        setup_body,
        out_shape=jax.ShapeDtypeStruct((dirs + 2, 2 * LANES, LANES), jnp.bfloat16),
        cost_estimate=cost(64),
        compiler_params=params(),
        name="setup",
    )()
    e1, e2, ya, yb = pl.pallas_call(
        functools.partial(pack_body, dirs),
        out_shape=(tile,) * 4,
        in_specs=[any_spec] + [vmem_spec] * 5,
        compiler_params=params(),
        name="pack",
    )(mats, *fields)
    yb = lax.ppermute(yb, "gy", swap(count_y, 1))
    ya = lax.ppermute(ya, "gy", swap(count_y, 0))
    xa, xb, hm = pl.pallas_call(
        functools.partial(rows_body, dirs),
        out_shape=(message, message, shape(2, LAYERS, ROWS, LANES)),
        compiler_params=params(),
        name="rows",
    )(ya, yb, *fields)
    xb = lax.ppermute(xb, "gx", swap(count_x, 1))
    xa = lax.ppermute(xa, "gx", swap(count_x, 0))
    g1, g2, h1, h2, hy = pl.pallas_call(
        functools.partial(near_body, dirs),
        out_shape=(tile, tile, many, many, shape(2, LAYERS, EXT, LANES)),
        scratch_shapes=phase_scratch(16, 16),
        cost_estimate=cost(16),
        compiler_params=params(),
        name="near",
    )(mats, *fields, xa, hm, e1, e2, ya, yb)
    return pl.pallas_call(
        functools.partial(rest_body, dirs),
        out_shape=(tile, tile, many, many),
        out_specs=[pl.BlockSpec(memory_space=pltpu.HBM)] * 4,
        scratch_shapes=[tile_s, tile_s, many_s, many_s, pltpu.SemaphoreType.DMA((2, dirs + 1))] + phase_scratch(8, 8),
        cost_estimate=cost(8),
        compiler_params=params(),
        name="rest",
    )(mats, *fields, xb, hm, hy, g1, g2, h1, h2)


def solution(mesh):
    plane = P(None, "gx", "gy")
    stack = P(None, None, "gx", "gy")
    return jax.shard_map(
        shards,
        mesh=mesh,
        in_specs=(plane, plane, plane, stack, stack),
        out_specs=(plane, plane, stack, stack),
        check_vma=False,
    )
```

time: 36.8 us -> 33.7 us (0.916)
  the two profiles are of different devices: /device:TPU:24 before, /device:TPU:23 now
where the time goes in v3:
time: 33.7 us; the launch traced here: 33.4 us
  starting transfers between devices  13 us (39%)
  Pallas kernels  11.8 us (35%)
  waiting for transfers between devices  5.08 us (15%)
  local copies, waits for them, and re-layouts  2.86 us (8%)
  between operations  0.71 us (2%)
    ppermute x1, starting transfers between devices, shards(): yb = lax.ppermute(yb, 'gy', swap(count_y, 1))  6.34 us
    pallas_call x1, Pallas kernels, shards(): pl.pallas_call(functools.partial(near_body, dirs), out_shape=(tile, tile,...  5.97 us
    pallas_call x1, Pallas kernels, shards(): pl.pallas_call(functools.partial(rest_body, dirs), out_shape=(tile, tile,...  4.66 us
    unnamed x12, local copies, waits for them, and re-layouts  2.86 us
    ppermute x1, waiting for transfers between devices, shards(): xb = lax.ppermute(xb, 'gx', swap(count_x, 1))  2.82 us
    ppermute x1, starting transfers between devices, shards(): xb = lax.ppermute(xb, 'gx', swap(count_x, 1))  2.72 us
    ppermute x1, waiting for transfers between devices, shards(): yb = lax.ppermute(yb, 'gy', swap(count_y, 1))  2.26 us
    ppermute x1, starting transfers between devices, shards(): xa = lax.ppermute(xa, 'gx', swap(count_x, 0))  2.19 us
  transfers between devices with their start and end apart: 4, of which 2 were waited for; matrix products, arithmetic and copies ran while one was open for 0% of the time, Pallas kernels for 18%

profile of v3, /device:TPU:23, one launch (start us, length us, event | category | flops | bytes accessed | tf_op | source)
XLA Modules:
  0.0 33.4 jit_solution(12783086554385556001)
XLA Ops:
  0.6 0.0 copy-start
  0.6 0.0 copy-start.4
  0.7 0.0 copy-start.3
  0.7 0.1 setup.1.first.mats
  0.8 0.9 %copy-done = f32[10,8,16,128]{3,2,1,0:T(8,128)S(1)} copy-done((f32[10,8,16,128]{3,2,1,0:T(8,128)S(1)}, f32[10,8,16,128]{3,2,1,0:T(8,128)}, u32[]{:S(2)}) %copy-start) | copy-done | bytes 655384
  1.7 0.0 copy-done.4
  1.7 0.0 copy-done.3
  1.7 0.0 copy-start.1
  1.7 1.1 %copy-done.1 = f32[10,8,16,128]{3,2,1,0:T(8,128)S(1)} copy-done((f32[10,8,16,128]{3,2,1,0:T(8,128)S(1)}, f32[10,8,16,128]{3,2,1,0:T(8,128)}, u32[]{:S(2)}) %copy-start.1) | copy-done | bytes 655384
  2.8 0.0 copy-start.5
  2.8 0.8 %copy-done.5 = f32[8,16,128]{2,1,0:T(8,128)S(1)} copy-done((f32[8,16,128]{2,1,0:T(8,128)S(1)}, f32[8,16,128]{2,1,0:T(8,128)}, u32[]{:S(2)}) %copy-start.5) | copy-done | bytes 65560
  3.7 0.0 copy-start.2
  3.7 0.9 %pack.1 = (f32[8,16,128]{2,1,0:T(8,128)S(1)}, f32[8,16,128]{2,1,0:T(8,128)S(1)}, f32[8,16,128]{2,1,0:T(8,128)S(1)}, f32[8,16,128]{2,1,0:T(8,128)S(1)}) custom-call(bf16[12,256,128]{2,1,0:T(8,128)(2,1)S(1)} %setup.1.first.mats, f32[8,16,128]{2,1,0:T(8,128)S(1)} %copy-done.3, f32[8,16,128]{2,1,0:T(8,128)S(1)} %copy-done.4, f32[8,16,128]{2,1,0:T(8,128)S(1)} %copy-done.5, ...), custom_call_target="tpu_custom_call" | custom-call | tf_op jit(solution)/shard_map/pack/pallas_call | solution.py:413
  4.5 1.7 %collective-permute-start = (f32[8,16,128]{2,1,0:T(8,128)S(1)}, f32[8,16,128]{2,1,0:T(8,128)S(1)}, u32[]{:S(2)}, u32[]{:S(2)}) collective-permute-start(f32[8,16,128]{2,1,0:T(8,128)S(1)} %get-tuple-element.16), channel_id=1, source_target_pairs={{0,1},{1,0},{2,3},{3,2},{4,5},{5,4},{6,7},{7,6},{8,9},{9,8},{10,11... | collective-permute-start | bytes 196616 | tf_op jit(solution)/shard_map/ppermute | solution.py:421
  6.3 6.3 %collective-permute-start.1 = (f32[8,16,128]{2,1,0:T(8,128)S(1)}, f32[8,16,128]{2,1,0:T(8,128)S(1)}, u32[]{:S(2)}, u32[]{:S(2)}) collective-permute-start(f32[8,16,128]{2,1,0:T(8,128)S(1)} %get-tuple-element.17), channel_id=1, source_target_pairs={{1,2},{2,1},{3,4},{4,3},{5,6},{6,5},{7,8},{8,7},{9,10},{10,9},{11,... | collective-permute-start | bytes 196616 | tf_op jit(solution)/shard_map/ppermute | solution.py:420
  12.6 0.0 collective-permute-done.ya
  12.6 2.3 %collective-permute-done.1.yb = f32[8,16,128]{2,1,0:T(8,128)S(1)} collective-permute-done((f32[8,16,128]{2,1,0:T(8,128)S(1)}, f32[8,16,128]{2,1,0:T(8,128)S(1)}, u32[]{:S(2)}, u32[]{:S(2)}) %collective-permute-start.1) | collective-permute-done | bytes 65568 | tf_op jit(solution)/shard_map/ppermute | solution.py:420
  14.9 0.0 copy-done.2
  14.9 0.2 rows.1
  15.0 2.2 %collective-permute-start.3 = (f32[13,8,8,128]{3,2,1,0:T(8,128)S(1)}, f32[13,8,8,128]{3,2,1,0:T(8,128)S(1)}, u32[]{:S(2)}, u32[]{:S(2)}) collective-permute-start(f32[13,8,8,128]{3,2,1,0:T(8,128)S(1)} %get-tuple-element.20), channel_id=1, source_target_pairs={{0,16},{16,0},{32,48},{48,32},{64,80},{80,64},{96,112},{112,96},{1... | collective-permute-start | bytes 1277960 | tf_op jit(solution)/shard_map/ppermute | solution.py:429
  17.2 2.7 %collective-permute-start.2 = (f32[13,8,8,128]{3,2,1,0:T(8,128)S(1)}, f32[13,8,8,128]{3,2,1,0:T(8,128)S(1)}, u32[]{:S(2)}, u32[]{:S(2)}) collective-permute-start(f32[13,8,8,128]{3,2,1,0:T(8,128)S(1)} %get-tuple-element.18), channel_id=1, source_target_pairs={{16,32},{32,16},{48,64},{64,48},{80,96},{96,80},{112,128},{128,112... | collective-permute-start | bytes 1277960 | tf_op jit(solution)/shard_map/ppermute | solution.py:428
  20.0 0.0 collective-permute-done.3.xa
  20.0 6.0 %near.1 = (f32[8,16,128]{2,1,0:T(8,128)S(1)}, f32[8,16,128]{2,1,0:T(8,128)S(1)}, f32[10,8,16,128]{3,2,1,0:T(8,128)S(1)}, f32[10,8,16,128]{3,2,1,0:T(8,128)S(1)}, f32[2,8,32,128]{3,2,1,0:T(8,128)S(1)}) custom-call(bf16[12,256,128]{2,1,0:T(8,128)(2,1)S(1)} %setup.1.first.mats, f32[8,16,128]{2,1,0:T(8,128)S(1)} %copy-done.3, f32[8,16,128]{2,1,0:T(8,128)S(1)} %copy-done.4, ...), custom_call_target="tpu_custom_call" | custom-call | bytes 16777216 | tf_op jit(solution)/shard_map/near/pallas_call | solution.py:430
  25.9 2.8 %collective-permute-done.2.xb = f32[13,8,8,128]{3,2,1,0:T(8,128)S(1)} collective-permute-done((f32[13,8,8,128]{3,2,1,0:T(8,128)S(1)}, f32[13,8,8,128]{3,2,1,0:T(8,128)S(1)}, u32[]{:S(2)}, u32[]{:S(2)}) %collective-permute-start.2) | collective-permute-done | bytes 426016 | tf_op jit(solution)/shard_map/ppermute | solution.py:428
  28.8 4.7 %rest.1 = (f32[8,16,128]{2,1,0:T(8,128)}, f32[8,16,128]{2,1,0:T(8,128)}, f32[10,8,16,128]{3,2,1,0:T(8,128)}, f32[10,8,16,128]{3,2,1,0:T(8,128)}) custom-call(bf16[12,256,128]{2,1,0:T(8,128)(2,1)S(1)} %setup.1.first.mats, f32[8,16,128]{2,1,0:T(8,128)S(1)} %copy-done.3, f32[8,16,128]{2,1,0:T(8,128)S(1)} %copy-done.4, f32[8,16,128]{2,1,0:T(8,128)S(1)} %copy-done.5, ...), custom_call_target="tpu_custom_call" | custom-call | bytes 8388608 | tf_op jit(solution)/shard_map/rest/pallas_call | solution.py:438
Async XLA Ops:
  0.6 1.1 %copy-start = (f32[10,8,16,128]{3,2,1,0:T(8,128)S(1)}, f32[10,8,16,128]{3,2,1,0:T(8,128)}, u32[]{:S(2)}) copy-start(f32[10,8,16,128]{3,2,1,0:T(8,128)} %d1.7) | copy-start | bytes 1966084
  0.6 1.1 %copy-start.4 = (f32[8,16,128]{2,1,0:T(8,128)S(1)}, f32[8,16,128]{2,1,0:T(8,128)}, u32[]{:S(2)}) copy-start(f32[8,16,128]{2,1,0:T(8,128)} %m2.7) | copy-start | bytes 196612
  0.7 1.1 %copy-start.3 = (f32[8,16,128]{2,1,0:T(8,128)S(1)}, f32[8,16,128]{2,1,0:T(8,128)}, u32[]{:S(2)}) copy-start(f32[8,16,128]{2,1,0:T(8,128)} %m1.7) | copy-start | bytes 196612
  1.7 1.1 %copy-start.1 = (f32[10,8,16,128]{3,2,1,0:T(8,128)S(1)}, f32[10,8,16,128]{3,2,1,0:T(8,128)}, u32[]{:S(2)}) copy-start(f32[10,8,16,128]{3,2,1,0:T(8,128)} %d2.7) | copy-start | bytes 1966084
  2.8 0.8 %copy-start.5 = (f32[8,16,128]{2,1,0:T(8,128)S(1)}, f32[8,16,128]{2,1,0:T(8,128)}, u32[]{:S(2)}) copy-start(f32[8,16,128]{2,1,0:T(8,128)} %w.7) | copy-start | bytes 196612
  3.7 11.2 %copy-start.2 = (f32[10,8,16,128]{3,2,1,0:T(8,128)S(1)}, f32[10,8,16,128]{3,2,1,0:T(8,128)}, u32[]{:S(2)}) copy-start(f32[10,8,16,128]{3,2,1,0:T(8,128)} %d2.7) | copy-start | bytes 1966084
  4.5 8.1 %collective-permute-start = (f32[8,16,128]{2,1,0:T(8,128)S(1)}, f32[8,16,128]{2,1,0:T(8,128)S(1)}, u32[]{:S(2)}, u32[]{:S(2)}) collective-permute-start(f32[8,16,128]{2,1,0:T(8,128)S(1)} %get-tuple-element.16), channel_id=1, source_target_pairs={{0,1},{1,0},{2,3},{3,2},{4,5},{5,4},{6,7},{7,6},{8,9},{9,8},{10,11... | collective-permute-start | bytes 196616 | tf_op jit(solution)/shard_map/ppermute | solution.py:421
  6.3 8.6 %collective-permute-start.1 = (f32[8,16,128]{2,1,0:T(8,128)S(1)}, f32[8,16,128]{2,1,0:T(8,128)S(1)}, u32[]{:S(2)}, u32[]{:S(2)}) collective-permute-start(f32[8,16,128]{2,1,0:T(8,128)S(1)} %get-tuple-element.17), channel_id=1, source_target_pairs={{1,2},{2,1},{3,4},{4,3},{5,6},{6,5},{7,8},{8,7},{9,10},{10,9},{11,... | collective-permute-start | bytes 196616 | tf_op jit(solution)/shard_map/ppermute | solution.py:420
  15.0 4.9 %collective-permute-start.3 = (f32[13,8,8,128]{3,2,1,0:T(8,128)S(1)}, f32[13,8,8,128]{3,2,1,0:T(8,128)S(1)}, u32[]{:S(2)}, u32[]{:S(2)}) collective-permute-start(f32[13,8,8,128]{3,2,1,0:T(8,128)S(1)} %get-tuple-element.20), channel_id=1, source_target_pairs={{0,16},{16,0},{32,48},{48,32},{64,80},{80,64},{96,112},{112,96},{1... | collective-permute-start | bytes 1277960 | tf_op jit(solution)/shard_map/ppermute | solution.py:429
  17.2 11.5 %collective-permute-start.2 = (f32[13,8,8,128]{3,2,1,0:T(8,128)S(1)}, f32[13,8,8,128]{3,2,1,0:T(8,128)S(1)}, u32[]{:S(2)}, u32[]{:S(2)}) collective-permute-start(f32[13,8,8,128]{3,2,1,0:T(8,128)S(1)} %get-tuple-element.18), channel_id=1, source_target_pairs={{16,32},{32,16},{48,64},{64,48},{80,96},{96,80},{112,128},{128,112... | collective-permute-start | bytes 1277960 | tf_op jit(solution)/shard_map/ppermute | solution.py:428

commit v4 on v3

--- a/solution.py
+++ b/solution.py
@@ -12,6 +12,8 @@
 EXT = 32
 LANES = 128
 MIB = 1024 * 1024
+NEAR_SLOTS = 2
+REST_SLOTS = 5
 F32 = jnp.float32
 
 
@@ -50,7 +52,18 @@
     return pltpu.roll(value, amount % value.shape[-2], axis=value.ndim - 2)
 
 
-def pack_body(dirs, first, m1, m2, w, d1, d2, e1, e2, ya, yb):
+def split(dirs, fields):
+    return (
+        fields.at[dirs],
+        fields.at[2 * dirs + 1],
+        fields.at[2 * dirs + 2],
+        fields.at[pl.ds(0, dirs)],
+        fields.at[pl.ds(dirs + 1, dirs)],
+    )
+
+
+def pack_body(dirs, fields, e1, e2, ya, yb):
+    m1, m2, w, d1, d2 = split(dirs, fields)
     side = lax.rem(lax.axis_index("gy"), 2)
     block = lane((ROWS, LANES)) // 8
     low = (lane((ROWS, LANES)) % 8) < 4
@@ -87,18 +100,26 @@
     return left, right, lroll(left, -4), lroll(right, 4)
 
 
-def rows_body(dirs, ya, yb, m1, m2, w, d1, d2, xa, xb, hm):
-    core = lax.rem(lax.axis_index("gx"), 2)
+def rows_body(dirs, ya, yb, fields, xb, hm):
     low = (lane((ROWS, LANES)) % 8) < 4
     for layer in range(LAYERS):
         left, right, left2, right2 = sides(ya, yb, layer)
         hm[0, layer] = jnp.where(low, left, right)
         hm[1, layer] = jnp.where(low, left2, right2)
+    message_rows(dirs, lax.rem(lax.axis_index("gx"), 2), fields, hm, (xb, xb.at[pl.ds(dirs, 3)]))
+
+
+def message_rows(dirs, tail, fields, hm, out):
+    m1, m2, w, d1, d2 = split(dirs, fields)
     pairs = [(d1.at[d], d2.at[d]) for d in range(dirs)] + [(m1, m2), (w, w), (hm.at[0], hm.at[1])]
     for index, (one, two) in enumerate(pairs):
         for layer in range(LAYERS):
-            xa[index, layer] = edge_rows(one, two, 1 - core, layer)
-            xb[index, layer] = edge_rows(one, two, core, layer)
+            target = out[0].at[index] if index < dirs else out[1].at[index - dirs]
+            target[layer] = edge_rows(one, two, tail, layer)
+
+
+def core_body(dirs, fields, hm, xa, xa_rest):
+    message_rows(dirs, 1 - lax.rem(lax.axis_index("gx"), 2), fields, hm, (xa, xa_rest))
 
 
 def stencil(up2, up1, down1, down2):
@@ -114,12 +135,21 @@
     return stencil(lroll(value, -2), lroll(value, -1), lroll(value, 1), lroll(value, 2))
 
 
-def diff_z(ref, layer, start, rows):
-    def at(offset):
-        where = layer + offset
-        return ref[where, pl.ds(start, rows), :] if 0 <= where < LAYERS else None
-
-    up2, up1, down1, down2 = at(2), at(1), at(-1), at(-2)
+def layers_of(ref, start, rows):
+    held = {}
+
+    def at(layer):
+        if not 0 <= layer < LAYERS:
+            return None
+        if layer not in held:
+            held[layer] = ref[layer, pl.ds(start, rows), :]
+        return held[layer]
+
+    return at
+
+
+def diff_z(at, layer):
+    up2, up1, down1, down2 = at(layer + 2), at(layer + 1), at(layer - 1), at(layer - 2)
     if up1 is None:
         total = -8.0 * down1
     elif down1 is None:
@@ -172,7 +202,8 @@
         mats[block, start : start + 16, :] = edge_rows_matrix(block)
 
 
-def phase(dirs, rows, wide, first_row, mats, m1, m2, w, d1, d2, message, hm, hy, outs, done, refs):
+def phase(dirs, rows, wide, slots, first_row, after, mats, fields, message, hm, hy, outs, done, refs):
+    m1, m2, w, d1, d2 = split(dirs, fields)
     ext_refs, h_ext, w_ext, s1, s2, cor, ax, ay, az, lhs_f, lhs_a, res_f, res_a = refs
     start = first_row + 8
     flat = (LAYERS * rows, LANES)
@@ -201,38 +232,44 @@
         return (part(0) + part(1)) + part(2)
 
     def fill(ext, own, beside, layer):
-        ext[layer, 0:8, :] = beside
-        ext[layer, 8:24, :] = own[layer]
-        ext[layer, 24:32, :] = beside
-
-    def load_ext(slot, one, two, index):
+        ext[layer, pl.ds(pl.multiple_of(24 * after, 8), 8), :] = beside
+        if rows == ROWS:
+            ext[layer, 8:24, :] = own[layer]
+        else:
+            begin = pl.multiple_of(8 * after, 8)
+            ext[layer, pl.ds(begin + 8, 8), :] = own[layer, pl.ds(begin, 8), :]
+
+    def load_ext(slot, one, two, source):
         for layer in range(LAYERS):
-            beside = message[index, layer]
+            beside = source[layer]
             fill(ext_refs.at[slot, 0], one, beside, layer)
             fill(ext_refs.at[slot, 1], two, sroll(beside, 4), layer)
         for k in (0, 1):
             put(lhs_f.at[slot], k, ext_refs[slot, k, :, main, :].reshape(flat))
 
     for layer in range(LAYERS):
-        beside = message[dirs + 2, layer]
+        beside = message[1][2, layer]
         fill(h_ext.at[0], hm.at[0], beside, layer)
         fill(h_ext.at[1], hm.at[1], sroll(beside, 4), layer)
-        fill(w_ext, w, message[dirs + 1, layer], layer)
+        fill(w_ext, w, message[1][1, layer], layer)
     for k in (0, 1):
         put(lhs_f.at[0], k, h_ext[k, :, main, :].reshape(flat), True)
-    load_ext(0, m1, m2, dirs)
+    load_ext(0, m1, m2, message[1].at[0])
     multiply(lhs_f.at[0], res_f.at[0], dirs, 0)
     multiply(lhs_f.at[0], res_f.at[0], dirs + 1, 1)
-    for k in (0, 1):
-        put(lhs_f.at[1], k, h_ext[k, :, main, :].reshape(flat), True)
-
-    def slopes(slot, k, layer):
-        ext = ext_refs.at[slot, k]
+    for slot in range(1, slots):
+        for k in (0, 1):
+            put(lhs_f.at[slot], k, h_ext[k, :, main, :].reshape(flat), True)
+
+    def slopes(slot, k, layer, layers):
         return (
-            diff_x(ext, layer, start, rows),
+            diff_x(ext_refs.at[slot, k], layer, start, rows),
             column(res_f.at[slot], k, layer),
-            diff_z(ext, layer, start, rows),
+            diff_z(layers, layer),
         )
+
+    def loaded(slot):
+        return tuple(layers_of(ext_refs.at[slot, k], start, rows) for k in (0, 1))
 
     fold = -1.0 / 20736.0
     block = lane((rows, LANES)) // 8
@@ -241,12 +278,13 @@
     def spread(value, at):
         return jnp.take_along_axis(value, within + 8 * at, axis=1)
 
+    packed = tuple(layers_of(h_ext.at[k], start, rows) for k in (0, 1))
     for layer in range(LAYERS):
         first, second = (
             (
                 diff_x(h_ext.at[k], layer, start, rows),
                 hy[k, layer, main, :],
-                diff_z(h_ext.at[k], layer, start, rows),
+                diff_z(packed[k], layer),
             )
             for k in (0, 1)
         )
@@ -259,22 +297,27 @@
         rw = tuple(weight * (left_term[i] + right_term[i]) for i in range(3))
         cor[0, layer, :rows, :] = cross(two, rw)[1]
         cor[1, layer, :rows, :] = cross(rw, one)[1]
-    for slot in (0, 1):
+    for slot in range(slots):
         for k in (0, 1):
             put(lhs_a.at[slot], k, cor[k, :, 2 : 2 + wide, :].reshape(flat_out), True)
 
+    models = loaded(0)
     for layer in range(LAYERS):
         for k, ref in ((0, s1), (1, s2)):
-            for index, part in enumerate(slopes(0, k, layer)):
+            for index, part in enumerate(slopes(0, k, layer, models[k])):
                 ref[index, layer] = part
 
     def products(slot, second_field):
+        held = loaded(slot)
         for layer in range(LAYERS):
             one = (s1[0, layer], s1[1, layer], s1[2, layer])
             two = (s2[0, layer], s2[1, layer], s2[2, layer])
             if second_field:
                 perturbed = tuple(
-                    p + q for p, q in zip(cross(slopes(slot, 0, layer), two), cross(one, slopes(slot, 1, layer)))
+                    p + q
+                    for p, q in zip(
+                        cross(slopes(slot, 0, layer, held[0]), two), cross(one, slopes(slot, 1, layer, held[1]))
+                    )
                 )
             else:
                 perturbed = cross(one, two)
@@ -289,11 +332,12 @@
 
     def divergence(slot, targets):
         for k in (0, 1):
+            layers = layers_of(az.at[slot, k], 2, wide)
             for layer in range(LAYERS):
                 total = (
                     diff_x(ax.at[slot, k], layer, 2, wide)
                     + column(res_a.at[slot], k, layer)
-                    + diff_z(az.at[slot, k], layer, 2, wide)
+                    + diff_z(layers, layer)
                 )
                 targets[k][layer, pl.ds(first_row + 2, rows - 4), :] = total[: rows - 4]
 
@@ -303,36 +347,38 @@
     divergence(0, (g1, g2))
     done(None)
 
-    @pl.loop(0, dirs // 2)
+    def batch(begin, count):
+        for slot in range(count):
+            load_ext(slot, d1.at[begin + slot], d2.at[begin + slot], message[0].at[begin + slot])
+            multiply(lhs_f.at[slot], res_f.at[slot], begin + slot)
+        for slot in range(count):
+            products(slot, True)
+            multiply(lhs_a.at[slot], res_a.at[slot], begin + slot)
+        for slot in range(count):
+            divergence(slot, (h1.at[begin + slot], h2.at[begin + slot]))
+            done(begin + slot)
+
+    @pl.loop(0, dirs // slots)
     def _(step):
-        d, e = 2 * step, 2 * step + 1
-        load_ext(0, d1.at[d], d2.at[d], d)
-        multiply(lhs_f.at[0], res_f.at[0], d)
-        load_ext(1, d1.at[e], d2.at[e], e)
-        multiply(lhs_f.at[1], res_f.at[1], e)
-        products(0, True)
-        multiply(lhs_a.at[0], res_a.at[0], d)
-        products(1, True)
-        multiply(lhs_a.at[1], res_a.at[1], e)
-        divergence(0, (h1.at[d], h2.at[d]))
-        divergence(1, (h1.at[e], h2.at[e]))
-        done(d)
-        done(e)
-
-
-def phase_scratch(rows, wide):
+        batch(step * slots, slots)
+
+    if dirs % slots:
+        batch(dirs - dirs % slots, dirs % slots)
+
+
+def phase_scratch(rows, wide, slots):
     ext = scratch(LAYERS, EXT, LANES)
     slopes = scratch(3, LAYERS, rows, LANES)
-    adjoint = scratch(2, 2, LAYERS, rows + 16, LANES)
+    adjoint = scratch(slots, 2, LAYERS, rows + 16, LANES)
     return [
-        scratch(2, 2, LAYERS, EXT, LANES), scratch(2, LAYERS, EXT, LANES), ext, slopes, slopes,
+        scratch(slots, 2, LAYERS, EXT, LANES), scratch(2, LAYERS, EXT, LANES), ext, slopes, slopes,
         scratch(2, LAYERS, rows + 16, LANES), adjoint, adjoint, adjoint,
-        half(2, 6 * LAYERS * rows, 2 * LANES), half(2, 6 * LAYERS * wide, 2 * LANES),
-        scratch(2, 6 * LAYERS * rows, LANES), scratch(2, 6 * LAYERS * wide, LANES),
+        half(slots, 6 * LAYERS * rows, 2 * LANES), half(slots, 6 * LAYERS * wide, 2 * LANES),
+        scratch(slots, 6 * LAYERS * rows, LANES), scratch(slots, 6 * LAYERS * wide, LANES),
     ]
 
 
-def near_body(dirs, mats, m1, m2, w, d1, d2, xa, hm, e1, e2, ya, yb, g1, g2, h1, h2, hy, *refs):
+def near_body(dirs, mats, fields, xa, xa_rest, hm, e1, e2, ya, yb, g1, g2, h1, h2, hy, *refs):
     core = lax.rem(lax.axis_index("gx"), 2)
     low = (lane((ROWS, LANES)) % 8) < 4
     for layer in range(LAYERS):
@@ -344,12 +390,12 @@
             hy[k, layer, 0:8, :] = jnp.zeros((8, LANES), F32)
             hy[k, layer, 24:32, :] = jnp.zeros((8, LANES), F32)
     phase(
-        dirs, 16, 16, 2 - 4 * core, mats, m1, m2, w, d1, d2, xa, hm, hy, (g1, g2, h1, h2), lambda d: None, refs
+        dirs, 16, 16, NEAR_SLOTS, 2 - 4 * core, 1 - core, mats, fields, (xa, xa_rest), hm, hy, (g1, g2, h1, h2), lambda d: None, refs
     )
 
 
 def rest_body(
-    dirs, mats, m1, m2, w, d1, d2, xb, hm, hy, g1_in, g2_in, h1_in, h2_in,
+    dirs, mats, fields, xb, hm, hy, g1_in, g2_in, h1_in, h2_in,
     g1_out, g2_out, h1_out, h2_out, g1, g2, h1, h2, sems, *refs,
 ):
     core = lax.rem(lax.axis_index("gx"), 2)
@@ -373,7 +419,7 @@
     g2[...] = g2_in[...]
     h1[...] = h1_in[...]
     h2[...] = h2_in[...]
-    phase(dirs, 8, 8, 12 * core - 2, mats, m1, m2, w, d1, d2, xb, hm, hy, (g1, g2, h1, h2), done, refs)
+    phase(dirs, 8, 8, REST_SLOTS, 12 * core - 2, core, mats, fields, (xb, xb.at[pl.ds(dirs, 3)]), hm, hy, (g1, g2, h1, h2), done, refs)
 
     @pl.loop(0, dirs)
     def _(d):
@@ -397,12 +443,13 @@
     tile = shape(LAYERS, ROWS, LANES)
     many = shape(dirs, LAYERS, ROWS, LANES)
     message = shape(dirs + 3, LAYERS, 8, LANES)
+    many_rows, few_rows = shape(dirs, LAYERS, 8, LANES), shape(3, LAYERS, 8, LANES)
     tile_s = scratch(LAYERS, ROWS, LANES)
     many_s = scratch(dirs, LAYERS, ROWS, LANES)
-    fields = (model_one, model_two, weight, direction_one, direction_two)
+    fields = jnp.concatenate(
+        [direction_one, model_one[None], direction_two, model_two[None], weight[None]], 0
+    )
     count_x, count_y = lax.axis_size("gx"), lax.axis_size("gy")
-    any_spec = pl.BlockSpec(memory_space=pl.ANY)
-    vmem_spec = pl.BlockSpec(memory_space=pltpu.VMEM)
     mats = pl.pallas_call(
         setup_body,
         out_shape=jax.ShapeDtypeStruct((dirs + 2, 2 * LANES, LANES), jnp.bfloat16),
@@ -413,37 +460,44 @@
     e1, e2, ya, yb = pl.pallas_call(
         functools.partial(pack_body, dirs),
         out_shape=(tile,) * 4,
-        in_specs=[any_spec] + [vmem_spec] * 5,
         compiler_params=params(),
         name="pack",
-    )(mats, *fields)
+    )(fields)
     yb = lax.ppermute(yb, "gy", swap(count_y, 1))
     ya = lax.ppermute(ya, "gy", swap(count_y, 0))
-    xa, xb, hm = pl.pallas_call(
+    xb, hm = pl.pallas_call(
         functools.partial(rows_body, dirs),
-        out_shape=(message, message, shape(2, LAYERS, ROWS, LANES)),
+        out_shape=(message, shape(2, LAYERS, ROWS, LANES)),
         compiler_params=params(),
         name="rows",
-    )(ya, yb, *fields)
+    )(ya, yb, fields)
     xb = lax.ppermute(xb, "gx", swap(count_x, 1))
+    xa, xa_rest = pl.pallas_call(
+        functools.partial(core_body, dirs),
+        out_shape=(many_rows, few_rows),
+        cost_estimate=cost(4),
+        compiler_params=params(),
+        name="core",
+    )(fields, hm)
     xa = lax.ppermute(xa, "gx", swap(count_x, 0))
+    xa_rest = lax.ppermute(xa_rest, "gx", swap(count_x, 0))
     g1, g2, h1, h2, hy = pl.pallas_call(
         functools.partial(near_body, dirs),
         out_shape=(tile, tile, many, many, shape(2, LAYERS, EXT, LANES)),
-        scratch_shapes=phase_scratch(16, 16),
+        scratch_shapes=phase_scratch(16, 16, NEAR_SLOTS),
         cost_estimate=cost(16),
         compiler_params=params(),
         name="near",
-    )(mats, *fields, xa, hm, e1, e2, ya, yb)
+    )(mats, fields, xa, xa_rest, hm, e1, e2, ya, yb)
     return pl.pallas_call(
         functools.partial(rest_body, dirs),
         out_shape=(tile, tile, many, many),
         out_specs=[pl.BlockSpec(memory_space=pltpu.HBM)] * 4,
-        scratch_shapes=[tile_s, tile_s, many_s, many_s, pltpu.SemaphoreType.DMA((2, dirs + 1))] + phase_scratch(8, 8),
+        scratch_shapes=[tile_s, tile_s, many_s, many_s, pltpu.SemaphoreType.DMA((2, dirs + 1))] + phase_scratch(8, 8, REST_SLOTS),
         cost_estimate=cost(8),
         compiler_params=params(),
         name="rest",
-    )(mats, *fields, xb, hm, hy, g1, g2, h1, h2)
+    )(mats, fields, xb, hm, hy, g1, g2, h1, h2)
 
 
 def solution(mesh):

time: 33.7 us -> 31.9 us (0.947)
  the two profiles are of different devices: /device:TPU:23 before, /device:TPU:29 now
where the time goes in v4:
time: 31.9 us; the launch traced here: 31.7 us
  starting transfers between devices  15.2 us (48%)
  Pallas kernels  10.9 us (34%)
  waiting for transfers between devices  2.76 us (9%)
  local copies, waits for them, and re-layouts  2.12 us (7%)
  between operations  0.77 us (2%)
    ppermute x1, starting transfers between devices, shards(): yb = lax.ppermute(yb, 'gy', swap(count_y, 1))  7.23 us
    pallas_call x1, Pallas kernels, shards(): pl.pallas_call(functools.partial(near_body, dirs), out_shape=(tile, tile,...  5.89 us
    ppermute x1, starting transfers between devices, shards(): xb = lax.ppermute(xb, 'gx', swap(count_x, 1))  5.69 us
    pallas_call x1, Pallas kernels, shards(): pl.pallas_call(functools.partial(rest_body, dirs), out_shape=(tile, tile,...  3.75 us
    unnamed x10, local copies, waits for them, and re-layouts  2.11 us
    ppermute x1, starting transfers between devices, shards(): ya = lax.ppermute(ya, 'gy', swap(count_y, 0))  1.72 us
    ppermute x1, waiting for transfers between devices, shards(): yb = lax.ppermute(yb, 'gy', swap(count_y, 1))  1.63 us
    ppermute x1, waiting for transfers between devices, shards(): xa_rest = lax.ppermute(xa_rest, 'gx', swap(count_x, 0))  1.12 us
  transfers between devices with their start and end apart: 5, of which 2 were waited for; matrix products, arithmetic and copies ran while one was open for 0% of the time, Pallas kernels for 19%

profile of v4, /device:TPU:29, one launch (start us, length us, event | category | flops | bytes accessed | tf_op | source)
XLA Modules:
  0.0 31.7 jit_solution(4542689071953088537)
XLA Ops:
  0.6 0.0 copy-start
  0.6 0.0 copy-start.1
  0.7 0.0 copy-start.2
  0.7 1.2 %constant_dynamic-update-slice_fusion.1 = f32[23,8,16,128]{3,2,1,0:T(8,128)S(1)} fusion(f32[10,8,16,128]{3,2,1,0:T(8,128)} %param.8), kind=kLoop, calls=%fused_computation.4 | loop fusion | bytes 1310720
  1.9 0.8 %bitcast_dynamic-update-slice_fusion.2 = f32[23,8,16,128]{3,2,1,0:T(8,128)S(1)} fusion(f32[23,8,16,128]{3,2,1,0:T(8,128)S(1)} %constant_dynamic-update-slice_fusion.1, f32[8,16,128]{2,1,0:T(8,128)} %param.5), kind=kLoop, calls=%fused_computation.2 | loop fusion | bytes 131072
  2.7 0.0 copy-done
  2.8 0.0 copy-done.1
  2.8 0.0 copy-done.2
  2.8 0.9 %pack.1 = (f32[8,16,128]{2,1,0:T(8,128)S(1)}, f32[8,16,128]{2,1,0:T(8,128)S(1)}, f32[8,16,128]{2,1,0:T(8,128)S(1)}, f32[8,16,128]{2,1,0:T(8,128)S(1)}) custom-call(f32[23,8,16,128]{3,2,1,0:T(8,128)S(1)} %bitcast_dynamic-update-slice_fusion.fields), custom_call_target="tpu_custom_call" | custom-call | tf_op jit(solution)/shard_map/pack/pallas_call | solution.py:460
  3.7 1.7 %collective-permute-start = (f32[8,16,128]{2,1,0:T(8,128)S(1)}, f32[8,16,128]{2,1,0:T(8,128)S(1)}, u32[]{:S(2)}, u32[]{:S(2)}) collective-permute-start(f32[8,16,128]{2,1,0:T(8,128)S(1)} %get-tuple-element.17), channel_id=1, source_target_pairs={{0,1},{1,0},{2,3},{3,2},{4,5},{5,4},{6,7},{7,6},{8,9},{9,8},{10,11... | collective-permute-start | bytes 196616 | tf_op jit(solution)/shard_map/ppermute | solution.py:467
  5.4 7.2 %collective-permute-start.1 = (f32[8,16,128]{2,1,0:T(8,128)S(1)}, f32[8,16,128]{2,1,0:T(8,128)S(1)}, u32[]{:S(2)}, u32[]{:S(2)}) collective-permute-start(f32[8,16,128]{2,1,0:T(8,128)S(1)} %get-tuple-element.18), channel_id=1, source_target_pairs={{1,2},{2,1},{3,4},{4,3},{5,6},{6,5},{7,8},{8,7},{9,10},{10,9},{11,... | collective-permute-start | bytes 196616 | tf_op jit(solution)/shard_map/ppermute | solution.py:466
  12.7 0.0 collective-permute-done.ya
  12.7 1.6 %collective-permute-done.1.yb = f32[8,16,128]{2,1,0:T(8,128)S(1)} collective-permute-done((f32[8,16,128]{2,1,0:T(8,128)S(1)}, f32[8,16,128]{2,1,0:T(8,128)S(1)}, u32[]{:S(2)}, u32[]{:S(2)}) %collective-permute-start.1) | collective-permute-done | bytes 65568 | tf_op jit(solution)/shard_map/ppermute | solution.py:466
  14.3 0.1 rows.1
  14.4 5.7 %collective-permute-start.2 = (f32[13,8,8,128]{3,2,1,0:T(8,128)S(1)}, f32[13,8,8,128]{3,2,1,0:T(8,128)S(1)}, u32[]{:S(2)}, u32[]{:S(2)}) collective-permute-start(f32[13,8,8,128]{3,2,1,0:T(8,128)S(1)} %get-tuple-element.19), channel_id=1, source_target_pairs={{16,32},{32,16},{48,64},{64,48},{80,96},{96,80},{112,128},{128,112... | collective-permute-start | bytes 1277960 | tf_op jit(solution)/shard_map/ppermute | solution.py:474
  20.1 0.1 core.1
  20.2 0.1 collective-permute-start.3
  20.3 0.5 %collective-permute-start.4 = (f32[3,8,8,128]{3,2,1,0:T(8,128)S(1)}, f32[3,8,8,128]{3,2,1,0:T(8,128)S(1)}, u32[]{:S(2)}, u32[]{:S(2)}) collective-permute-start(f32[3,8,8,128]{3,2,1,0:T(8,128)S(1)} %get-tuple-element.22), channel_id=1, source_target_pairs={{0,16},{16,0},{32,48},{48,32},{64,80},{80,64},{96,112},{112,96},{1... | collective-permute-start | bytes 294920 | tf_op jit(solution)/shard_map/ppermute | solution.py:483
  20.8 0.1 setup.1.mats
  20.9 1.1 %collective-permute-done.4.xa_rest = f32[3,8,8,128]{3,2,1,0:T(8,128)S(1)} collective-permute-done((f32[3,8,8,128]{3,2,1,0:T(8,128)S(1)}, f32[3,8,8,128]{3,2,1,0:T(8,128)S(1)}, u32[]{:S(2)}, u32[]{:S(2)}) %collective-permute-start.4) | collective-permute-done | bytes 98336 | tf_op jit(solution)/shard_map/ppermute | solution.py:483
  22.1 0.0 collective-permute-done.3.xa
  22.1 5.9 %near.1 = (f32[8,16,128]{2,1,0:T(8,128)S(1)}, f32[8,16,128]{2,1,0:T(8,128)S(1)}, f32[10,8,16,128]{3,2,1,0:T(8,128)S(1)}, f32[10,8,16,128]{3,2,1,0:T(8,128)S(1)}, f32[2,8,32,128]{3,2,1,0:T(8,128)S(1)}) custom-call(bf16[12,256,128]{2,1,0:T(8,128)(2,1)S(1)} %setup.1.mats, f32[23,8,16,128]{3,2,1,0:T(8,128)S(1)} %bitcast_dynamic-update-slice_fusion.fields, ...), custom_call_target="tpu_custom_call" | custom-call | bytes 16777216 | tf_op jit(solution)/shard_map/near/pallas_call | solution.py:484
  28.0 0.0 collective-permute-done.2.xb
  28.0 3.7 %rest.1 = (f32[8,16,128]{2,1,0:T(8,128)}, f32[8,16,128]{2,1,0:T(8,128)}, f32[10,8,16,128]{3,2,1,0:T(8,128)}, f32[10,8,16,128]{3,2,1,0:T(8,128)}) custom-call(bf16[12,256,128]{2,1,0:T(8,128)(2,1)S(1)} %setup.1.mats, f32[23,8,16,128]{3,2,1,0:T(8,128)S(1)} %bitcast_dynamic-update-slice_fusion.fields, f32[13,8,8,128]{3,2,1,0:T(8,128)S(1)} %collective-permute-done.2.xb, ...), custom_call_target="tpu_custom_call" | custom-call | bytes 8388608 | tf_op jit(solution)/shard_map/rest/pallas_call | solution.py:492
  (3 shorter events, 0.1 us)
Async XLA Ops:
  0.6 2.1 %copy-start = (f32[10,8,16,128]{3,2,1,0:T(8,128)S(1)}, f32[10,8,16,128]{3,2,1,0:T(8,128)}, u32[]{:S(2)}) copy-start(f32[10,8,16,128]{3,2,1,0:T(8,128)} %param.9) | copy-start | bytes 1966084
  0.6 2.1 %copy-start.1 = (f32[8,16,128]{2,1,0:T(8,128)S(1)}, f32[8,16,128]{2,1,0:T(8,128)}, u32[]{:S(2)}) copy-start(f32[8,16,128]{2,1,0:T(8,128)} %param.6) | copy-start | bytes 196612
  0.7 2.1 %copy-start.2 = (f32[8,16,128]{2,1,0:T(8,128)S(1)}, f32[8,16,128]{2,1,0:T(8,128)}, u32[]{:S(2)}) copy-start(f32[8,16,128]{2,1,0:T(8,128)} %param.7) | copy-start | bytes 196612
  3.7 9.0 %collective-permute-start = (f32[8,16,128]{2,1,0:T(8,128)S(1)}, f32[8,16,128]{2,1,0:T(8,128)S(1)}, u32[]{:S(2)}, u32[]{:S(2)}) collective-permute-start(f32[8,16,128]{2,1,0:T(8,128)S(1)} %get-tuple-element.17), channel_id=1, source_target_pairs={{0,1},{1,0},{2,3},{3,2},{4,5},{5,4},{6,7},{7,6},{8,9},{9,8},{10,11... | collective-permute-start | bytes 196616 | tf_op jit(solution)/shard_map/ppermute | solution.py:467
  5.4 8.9 %collective-permute-start.1 = (f32[8,16,128]{2,1,0:T(8,128)S(1)}, f32[8,16,128]{2,1,0:T(8,128)S(1)}, u32[]{:S(2)}, u32[]{:S(2)}) collective-permute-start(f32[8,16,128]{2,1,0:T(8,128)S(1)} %get-tuple-element.18), channel_id=1, source_target_pairs={{1,2},{2,1},{3,4},{4,3},{5,6},{6,5},{7,8},{8,7},{9,10},{10,9},{11,... | collective-permute-start | bytes 196616 | tf_op jit(solution)/shard_map/ppermute | solution.py:466
  14.4 13.5 %collective-permute-start.2 = (f32[13,8,8,128]{3,2,1,0:T(8,128)S(1)}, f32[13,8,8,128]{3,2,1,0:T(8,128)S(1)}, u32[]{:S(2)}, u32[]{:S(2)}) collective-permute-start(f32[13,8,8,128]{3,2,1,0:T(8,128)S(1)} %get-tuple-element.19), channel_id=1, source_target_pairs={{16,32},{32,16},{48,64},{64,48},{80,96},{96,80},{112,128},{128,112... | collective-permute-start | bytes 1277960 | tf_op jit(solution)/shard_map/ppermute | solution.py:474
  20.2 1.9 %collective-permute-start.3 = (f32[10,8,8,128]{3,2,1,0:T(8,128)S(1)}, f32[10,8,8,128]{3,2,1,0:T(8,128)S(1)}, u32[]{:S(2)}, u32[]{:S(2)}) collective-permute-start(f32[10,8,8,128]{3,2,1,0:T(8,128)S(1)} %get-tuple-element.21), channel_id=1, source_target_pairs={{0,16},{16,0},{32,48},{48,32},{64,80},{80,64},{96,112},{112,96},{1... | collective-permute-start | bytes 983048 | tf_op jit(solution)/shard_map/ppermute | solution.py:482
  20.3 1.8 %collective-permute-start.4 = (f32[3,8,8,128]{3,2,1,0:T(8,128)S(1)}, f32[3,8,8,128]{3,2,1,0:T(8,128)S(1)}, u32[]{:S(2)}, u32[]{:S(2)}) collective-permute-start(f32[3,8,8,128]{3,2,1,0:T(8,128)S(1)} %get-tuple-element.22), channel_id=1, source_target_pairs={{0,16},{16,0},{32,48},{48,32},{64,80},{80,64},{96,112},{112,96},{1... | collective-permute-start | bytes 294920 | tf_op jit(solution)/shard_map/ppermute | solution.py:483

commit v5 on v4

--- a/solution.py
+++ b/solution.py
@@ -12,8 +12,8 @@
 EXT = 32
 LANES = 128
 MIB = 1024 * 1024
-NEAR_SLOTS = 2
-REST_SLOTS = 5
+NEAR_SLOTS = 5
+REST_SLOTS = 10
 F32 = jnp.float32
 
 
@@ -206,18 +206,20 @@
     m1, m2, w, d1, d2 = split(dirs, fields)
     ext_refs, h_ext, w_ext, s1, s2, cor, ax, ay, az, lhs_f, lhs_a, res_f, res_a = refs
     start = first_row + 8
-    flat = (LAYERS * rows, LANES)
-    flat_out = (LAYERS * wide, LANES)
     main = pl.ds(start, rows)
 
     def put(lhs, index, value, right=False):
-        count = value.shape[0]
-        for at, part in enumerate(split3(value)):
-            begin = (3 * index + at) * count
-            if right:
-                lhs[begin : begin + count, LANES:] = part
-            else:
-                lhs[begin : begin + count, :LANES] = part
+        each = value.shape[1]
+        group = ROWS // each
+        count = LAYERS * each
+        for layer in range(0, LAYERS, group):
+            block = jnp.concatenate([value[layer + at] for at in range(group)], 0) if group > 1 else value[layer]
+            for at, part in enumerate(split3(block)):
+                begin = (3 * index + at) * count + layer * each
+                if right:
+                    lhs[begin : begin + ROWS, LANES:] = part
+                else:
+                    lhs[begin : begin + ROWS, :LANES] = part
 
     def multiply(lhs, result, block, index=None):
         each = lhs.shape[0] // 2
@@ -245,7 +247,7 @@
             fill(ext_refs.at[slot, 0], one, beside, layer)
             fill(ext_refs.at[slot, 1], two, sroll(beside, 4), layer)
         for k in (0, 1):
-            put(lhs_f.at[slot], k, ext_refs[slot, k, :, main, :].reshape(flat))
+            put(lhs_f.at[slot], k, ext_refs[slot, k, :, main, :])
 
     for layer in range(LAYERS):
         beside = message[1][2, layer]
@@ -253,13 +255,13 @@
         fill(h_ext.at[1], hm.at[1], sroll(beside, 4), layer)
         fill(w_ext, w, message[1][1, layer], layer)
     for k in (0, 1):
-        put(lhs_f.at[0], k, h_ext[k, :, main, :].reshape(flat), True)
+        put(lhs_f.at[0], k, h_ext[k, :, main, :], True)
     load_ext(0, m1, m2, message[1].at[0])
     multiply(lhs_f.at[0], res_f.at[0], dirs, 0)
     multiply(lhs_f.at[0], res_f.at[0], dirs + 1, 1)
     for slot in range(1, slots):
         for k in (0, 1):
-            put(lhs_f.at[slot], k, h_ext[k, :, main, :].reshape(flat), True)
+            put(lhs_f.at[slot], k, h_ext[k, :, main, :], True)
 
     def slopes(slot, k, layer, layers):
         return (
@@ -299,7 +301,7 @@
         cor[1, layer, :rows, :] = cross(rw, one)[1]
     for slot in range(slots):
         for k in (0, 1):
-            put(lhs_a.at[slot], k, cor[k, :, 2 : 2 + wide, :].reshape(flat_out), True)
+            put(lhs_a.at[slot], k, cor[k, :, 2 : 2 + wide, :], True)
 
     models = loaded(0)
     for layer in range(LAYERS):
@@ -328,7 +330,7 @@
                 ay[slot, k, layer, :rows, :] = adj[1]
                 az[slot, k, layer, :rows, :] = adj[2]
         for k in (0, 1):
-            put(lhs_a.at[slot], k, ay[slot, k, :, 2 : 2 + wide, :].reshape(flat_out))
+            put(lhs_a.at[slot], k, ay[slot, k, :, 2 : 2 + wide, :])
 
     def divergence(slot, targets):
         for k in (0, 1):
@@ -378,8 +380,7 @@
     ]
 
 
-def near_body(dirs, mats, fields, xa, xa_rest, hm, e1, e2, ya, yb, g1, g2, h1, h2, hy, *refs):
-    core = lax.rem(lax.axis_index("gx"), 2)
+def halo_body(e1, e2, ya, yb, hy):
     low = (lane((ROWS, LANES)) % 8) < 4
     for layer in range(LAYERS):
         left, right, left2, right2 = sides(ya, yb, layer)
@@ -389,6 +390,10 @@
             hy[k, layer, 8:24, :] = jnp.where(low, before, after)
             hy[k, layer, 0:8, :] = jnp.zeros((8, LANES), F32)
             hy[k, layer, 24:32, :] = jnp.zeros((8, LANES), F32)
+
+
+def near_body(dirs, mats, fields, xa, xa_rest, hm, hy, g1, g2, h1, h2, *refs):
+    core = lax.rem(lax.axis_index("gx"), 2)
     phase(
         dirs, 16, 16, NEAR_SLOTS, 2 - 4 * core, 1 - core, mats, fields, (xa, xa_rest), hm, hy, (g1, g2, h1, h2), lambda d: None, refs
     )
@@ -481,14 +486,21 @@
     )(fields, hm)
     xa = lax.ppermute(xa, "gx", swap(count_x, 0))
     xa_rest = lax.ppermute(xa_rest, "gx", swap(count_x, 0))
-    g1, g2, h1, h2, hy = pl.pallas_call(
+    hy = pl.pallas_call(
+        halo_body,
+        out_shape=shape(2, LAYERS, EXT, LANES),
+        cost_estimate=cost(2),
+        compiler_params=params(),
+        name="halo",
+    )(e1, e2, ya, yb)
+    g1, g2, h1, h2 = pl.pallas_call(
         functools.partial(near_body, dirs),
-        out_shape=(tile, tile, many, many, shape(2, LAYERS, EXT, LANES)),
+        out_shape=(tile, tile, many, many),
         scratch_shapes=phase_scratch(16, 16, NEAR_SLOTS),
         cost_estimate=cost(16),
         compiler_params=params(),
         name="near",
-    )(mats, fields, xa, xa_rest, hm, e1, e2, ya, yb)
+    )(mats, fields, xa, xa_rest, hm, hy)
     return pl.pallas_call(
         functools.partial(rest_body, dirs),
         out_shape=(tile, tile, many, many),

time: 31.9 us -> 31.2 us (0.978)
  the two profiles are of different devices: /device:TPU:29 before, /device:TPU:24 now
where the time goes in v5:
time: 31.2 us; the launch traced here: 30.7 us
  starting transfers between devices  13.2 us (42%)
  Pallas kernels  10.8 us (35%)
  waiting for transfers between devices  3.86 us (12%)
  local copies, waits for them, and re-layouts  2.12 us (7%)
  between operations  0.76 us (2%)
    ppermute x1, starting transfers between devices, shards(): yb = lax.ppermute(yb, 'gy', swap(count_y, 1))  7.51 us
    pallas_call x1, Pallas kernels, shards(): pl.pallas_call(functools.partial(near_body, dirs), out_shape=(tile, tile,...  5.4 us
    pallas_call x1, Pallas kernels, shards(): pl.pallas_call(functools.partial(rest_body, dirs), out_shape=(tile, tile,...  3.6 us
    ppermute x1, starting transfers between devices, shards(): xb = lax.ppermute(xb, 'gx', swap(count_x, 1))  2.85 us
    ppermute x1, waiting for transfers between devices, shards(): yb = lax.ppermute(yb, 'gy', swap(count_y, 1))  2.23 us
    unnamed x10, local copies, waits for them, and re-layouts  2.11 us
    ppermute x1, starting transfers between devices, shards(): ya = lax.ppermute(ya, 'gy', swap(count_y, 0))  2 us
    ppermute x1, waiting for transfers between devices, shards(): xb = lax.ppermute(xb, 'gx', swap(count_x, 1))  1.06 us
  transfers between devices with their start and end apart: 5, of which 3 were waited for; matrix products, arithmetic and copies ran while one was open for 0% of the time, Pallas kernels for 20%

profile of v5, /device:TPU:24, one launch (start us, length us, event | category | flops | bytes accessed | tf_op | source)
XLA Modules:
  0.0 30.7 jit_solution(11675242984642912787)
XLA Ops:
  0.6 0.0 copy-start
  0.6 0.0 copy-start.1
  0.7 0.0 copy-start.2
  0.7 1.2 %constant_dynamic-update-slice_fusion.1 = f32[23,8,16,128]{3,2,1,0:T(8,128)S(1)} fusion(f32[10,8,16,128]{3,2,1,0:T(8,128)} %param.8), kind=kLoop, calls=%fused_computation.4 | loop fusion | bytes 1310720
  1.9 0.8 %bitcast_dynamic-update-slice_fusion.2 = f32[23,8,16,128]{3,2,1,0:T(8,128)S(1)} fusion(f32[23,8,16,128]{3,2,1,0:T(8,128)S(1)} %constant_dynamic-update-slice_fusion.1, f32[8,16,128]{2,1,0:T(8,128)} %param.5), kind=kLoop, calls=%fused_computation.2 | loop fusion | bytes 131072
  2.7 0.0 copy-done
  2.8 0.0 copy-done.1
  2.8 0.0 copy-done.2
  2.8 0.9 %pack.1 = (f32[8,16,128]{2,1,0:T(8,128)S(1)}, f32[8,16,128]{2,1,0:T(8,128)S(1)}, f32[8,16,128]{2,1,0:T(8,128)S(1)}, f32[8,16,128]{2,1,0:T(8,128)S(1)}) custom-call(f32[23,8,16,128]{3,2,1,0:T(8,128)S(1)} %bitcast_dynamic-update-slice_fusion.fields), custom_call_target="tpu_custom_call" | custom-call | tf_op jit(solution)/shard_map/pack/pallas_call | solution.py:465
  3.7 2.0 %collective-permute-start = (f32[8,16,128]{2,1,0:T(8,128)S(1)}, f32[8,16,128]{2,1,0:T(8,128)S(1)}, u32[]{:S(2)}, u32[]{:S(2)}) collective-permute-start(f32[8,16,128]{2,1,0:T(8,128)S(1)} %get-tuple-element.16), channel_id=1, source_target_pairs={{0,1},{1,0},{2,3},{3,2},{4,5},{5,4},{6,7},{7,6},{8,9},{9,8},{10,11... | collective-permute-start | bytes 196616 | tf_op jit(solution)/shard_map/ppermute | solution.py:472
  5.7 7.5 %collective-permute-start.1 = (f32[8,16,128]{2,1,0:T(8,128)S(1)}, f32[8,16,128]{2,1,0:T(8,128)S(1)}, u32[]{:S(2)}, u32[]{:S(2)}) collective-permute-start(f32[8,16,128]{2,1,0:T(8,128)S(1)} %get-tuple-element.17), channel_id=1, source_target_pairs={{1,2},{2,1},{3,4},{4,3},{5,6},{6,5},{7,8},{8,7},{9,10},{10,9},{11,... | collective-permute-start | bytes 196616 | tf_op jit(solution)/shard_map/ppermute | solution.py:471
  13.2 0.0 collective-permute-done.ya
  13.2 2.2 %collective-permute-done.1.yb = f32[8,16,128]{2,1,0:T(8,128)S(1)} collective-permute-done((f32[8,16,128]{2,1,0:T(8,128)S(1)}, f32[8,16,128]{2,1,0:T(8,128)S(1)}, u32[]{:S(2)}, u32[]{:S(2)}) %collective-permute-start.1) | collective-permute-done | bytes 65568 | tf_op jit(solution)/shard_map/ppermute | solution.py:471
  15.5 0.1 rows.1
  15.6 2.9 %collective-permute-start.2 = (f32[13,8,8,128]{3,2,1,0:T(8,128)S(1)}, f32[13,8,8,128]{3,2,1,0:T(8,128)S(1)}, u32[]{:S(2)}, u32[]{:S(2)}) collective-permute-start(f32[13,8,8,128]{3,2,1,0:T(8,128)S(1)} %get-tuple-element.18), channel_id=1, source_target_pairs={{16,32},{32,16},{48,64},{64,48},{80,96},{96,80},{112,128},{128,112... | collective-permute-start | bytes 1277960 | tf_op jit(solution)/shard_map/ppermute | solution.py:479
  18.5 0.1 core.1
  18.5 0.7 %collective-permute-start.3 = (f32[10,8,8,128]{3,2,1,0:T(8,128)S(1)}, f32[10,8,8,128]{3,2,1,0:T(8,128)S(1)}, u32[]{:S(2)}, u32[]{:S(2)}) collective-permute-start(f32[10,8,8,128]{3,2,1,0:T(8,128)S(1)} %get-tuple-element.22), channel_id=1, source_target_pairs={{0,16},{16,0},{32,48},{48,32},{64,80},{80,64},{96,112},{112,96},{1... | collective-permute-start | bytes 983048 | tf_op jit(solution)/shard_map/ppermute | solution.py:487
  19.3 0.1 collective-permute-start.4
  19.4 0.1 setup.1.mats
  19.5 0.6 %halo.1.hy = f32[2,8,32,128]{3,2,1,0:T(8,128)S(1)} custom-call(f32[8,16,128]{2,1,0:T(8,128)S(1)} %get-tuple-element.20.e1, f32[8,16,128]{2,1,0:T(8,128)S(1)} %get-tuple-element.21.e2, f32[8,16,128]{2,1,0:T(8,128)S(1)} %collective-permute-done.ya, f32[8,16,128]{2,1,0:T(8,128)S(1)} %collective-permute-done.1.yb), custom_call_target="tpu_custom_call" | custom-call | bytes 2097152 | tf_op jit(solution)/shard_map/halo/pallas_call | solution.py:489
  20.1 0.6 %collective-permute-done.4.xa_rest = f32[3,8,8,128]{3,2,1,0:T(8,128)S(1)} collective-permute-done((f32[3,8,8,128]{3,2,1,0:T(8,128)S(1)}, f32[3,8,8,128]{3,2,1,0:T(8,128)S(1)}, u32[]{:S(2)}, u32[]{:S(2)}) %collective-permute-start.4) | collective-permute-done | bytes 98336 | tf_op jit(solution)/shard_map/ppermute | solution.py:488
  20.7 0.0 collective-permute-done.3.xa
  20.7 5.4 %near.1 = (f32[8,16,128]{2,1,0:T(8,128)S(1)}, f32[8,16,128]{2,1,0:T(8,128)S(1)}, f32[10,8,16,128]{3,2,1,0:T(8,128)S(1)}, f32[10,8,16,128]{3,2,1,0:T(8,128)S(1)}) custom-call(bf16[12,256,128]{2,1,0:T(8,128)(2,1)S(1)} %setup.1.mats, f32[23,8,16,128]{3,2,1,0:T(8,128)S(1)} %bitcast_dynamic-update-slice_fusion.fields, ...), custom_call_target="tpu_custom_call" | custom-call | bytes 16777216 | tf_op jit(solution)/shard_map/near/pallas_call | solution.py:496
  26.1 1.1 %collective-permute-done.2.xb = f32[13,8,8,128]{3,2,1,0:T(8,128)S(1)} collective-permute-done((f32[13,8,8,128]{3,2,1,0:T(8,128)S(1)}, f32[13,8,8,128]{3,2,1,0:T(8,128)S(1)}, u32[]{:S(2)}, u32[]{:S(2)}) %collective-permute-start.2) | collective-permute-done | bytes 426016 | tf_op jit(solution)/shard_map/ppermute | solution.py:479
  27.2 3.6 %rest.1 = (f32[8,16,128]{2,1,0:T(8,128)}, f32[8,16,128]{2,1,0:T(8,128)}, f32[10,8,16,128]{3,2,1,0:T(8,128)}, f32[10,8,16,128]{3,2,1,0:T(8,128)}) custom-call(bf16[12,256,128]{2,1,0:T(8,128)(2,1)S(1)} %setup.1.mats, f32[23,8,16,128]{3,2,1,0:T(8,128)S(1)} %bitcast_dynamic-update-slice_fusion.fields, f32[13,8,8,128]{3,2,1,0:T(8,128)S(1)} %collective-permute-done.2.xb, ...), custom_call_target="tpu_custom_call" | custom-call | bytes 8388608 | tf_op jit(solution)/shard_map/rest/pallas_call | solution.py:504
  (3 shorter events, 0.1 us)
Async XLA Ops:
  0.6 2.1 %copy-start = (f32[10,8,16,128]{3,2,1,0:T(8,128)S(1)}, f32[10,8,16,128]{3,2,1,0:T(8,128)}, u32[]{:S(2)}) copy-start(f32[10,8,16,128]{3,2,1,0:T(8,128)} %param.9) | copy-start | bytes 1966084
  0.6 2.1 %copy-start.1 = (f32[8,16,128]{2,1,0:T(8,128)S(1)}, f32[8,16,128]{2,1,0:T(8,128)}, u32[]{:S(2)}) copy-start(f32[8,16,128]{2,1,0:T(8,128)} %param.6) | copy-start | bytes 196612
  0.7 2.1 %copy-start.2 = (f32[8,16,128]{2,1,0:T(8,128)S(1)}, f32[8,16,128]{2,1,0:T(8,128)}, u32[]{:S(2)}) copy-start(f32[8,16,128]{2,1,0:T(8,128)} %param.7) | copy-start | bytes 196612
  3.7 9.5 %collective-permute-start = (f32[8,16,128]{2,1,0:T(8,128)S(1)}, f32[8,16,128]{2,1,0:T(8,128)S(1)}, u32[]{:S(2)}, u32[]{:S(2)}) collective-permute-start(f32[8,16,128]{2,1,0:T(8,128)S(1)} %get-tuple-element.16), channel_id=1, source_target_pairs={{0,1},{1,0},{2,3},{3,2},{4,5},{5,4},{6,7},{7,6},{8,9},{9,8},{10,11... | collective-permute-start | bytes 196616 | tf_op jit(solution)/shard_map/ppermute | solution.py:472
  5.7 9.8 %collective-permute-start.1 = (f32[8,16,128]{2,1,0:T(8,128)S(1)}, f32[8,16,128]{2,1,0:T(8,128)S(1)}, u32[]{:S(2)}, u32[]{:S(2)}) collective-permute-start(f32[8,16,128]{2,1,0:T(8,128)S(1)} %get-tuple-element.17), channel_id=1, source_target_pairs={{1,2},{2,1},{3,4},{4,3},{5,6},{6,5},{7,8},{8,7},{9,10},{10,9},{11,... | collective-permute-start | bytes 196616 | tf_op jit(solution)/shard_map/ppermute | solution.py:471
  15.6 11.6 %collective-permute-start.2 = (f32[13,8,8,128]{3,2,1,0:T(8,128)S(1)}, f32[13,8,8,128]{3,2,1,0:T(8,128)S(1)}, u32[]{:S(2)}, u32[]{:S(2)}) collective-permute-start(f32[13,8,8,128]{3,2,1,0:T(8,128)S(1)} %get-tuple-element.18), channel_id=1, source_target_pairs={{16,32},{32,16},{48,64},{64,48},{80,96},{96,80},{112,128},{128,112... | collective-permute-start | bytes 1277960 | tf_op jit(solution)/shard_map/ppermute | solution.py:479
  18.5 2.1 %collective-permute-start.3 = (f32[10,8,8,128]{3,2,1,0:T(8,128)S(1)}, f32[10,8,8,128]{3,2,1,0:T(8,128)S(1)}, u32[]{:S(2)}, u32[]{:S(2)}) collective-permute-start(f32[10,8,8,128]{3,2,1,0:T(8,128)S(1)} %get-tuple-element.22), channel_id=1, source_target_pairs={{0,16},{16,0},{32,48},{48,32},{64,80},{80,64},{96,112},{112,96},{1... | collective-permute-start | bytes 983048 | tf_op jit(solution)/shard_map/ppermute | solution.py:487
  19.3 1.4 %collective-permute-start.4 = (f32[3,8,8,128]{3,2,1,0:T(8,128)S(1)}, f32[3,8,8,128]{3,2,1,0:T(8,128)S(1)}, u32[]{:S(2)}, u32[]{:S(2)}) collective-permute-start(f32[3,8,8,128]{3,2,1,0:T(8,128)S(1)} %get-tuple-element.23), channel_id=1, source_target_pairs={{0,16},{16,0},{32,48},{48,32},{64,80},{80,64},{96,112},{112,96},{1... | collective-permute-start | bytes 294920 | tf_op jit(solution)/shard_map/ppermute | solution.py:488

commit v6 on v5

--- a/solution.py
+++ b/solution.py
@@ -54,11 +54,11 @@
 
 def split(dirs, fields):
     return (
-        fields.at[dirs],
+        fields.at[2 * dirs],
         fields.at[2 * dirs + 1],
         fields.at[2 * dirs + 2],
         fields.at[pl.ds(0, dirs)],
-        fields.at[pl.ds(dirs + 1, dirs)],
+        fields.at[pl.ds(dirs, dirs)],
     )
 
 
@@ -452,7 +452,7 @@
     tile_s = scratch(LAYERS, ROWS, LANES)
     many_s = scratch(dirs, LAYERS, ROWS, LANES)
     fields = jnp.concatenate(
-        [direction_one, model_one[None], direction_two, model_two[None], weight[None]], 0
+        [direction_one, direction_two, model_one[None], model_two[None], weight[None]], 0
     )
     count_x, count_y = lax.axis_size("gx"), lax.axis_size("gy")
     mats = pl.pallas_call(

time: 31.2 us -> 30.4 us (0.974)
  local copies, waits for them, and re-layouts: 2.12 us -> 1.32 us
    unnamed x10 -> x12, local copies, waits for them, and re-layouts: 2.11 us -> 1.31 us
  transfers between devices with their start and end apart: 5 -> 5, of which waited for: 3 -> 3; matrix products, arithmetic and copies ran while one was open for 0% -> 0% of each run, Pallas kernels for 20% -> 21%
where the time goes in v6:
time: 30.4 us; the launch traced here: 30 us
  starting transfers between devices  13.2 us (43%)
  Pallas kernels  10.8 us (36%)
  waiting for transfers between devices  3.87 us (13%)
  local copies, waits for them, and re-layouts  1.32 us (4%)
  between operations  0.78 us (3%)
    ppermute x1, starting transfers between devices, shards(): yb = lax.ppermute(yb, 'gy', swap(count_y, 1))  7.51 us
    pallas_call x1, Pallas kernels, shards(): pl.pallas_call(functools.partial(near_body, dirs), out_shape=(tile, tile,...  5.39 us
    pallas_call x1, Pallas kernels, shards(): pl.pallas_call(functools.partial(rest_body, dirs), out_shape=(tile, tile,...  3.6 us
    ppermute x1, starting transfers between devices, shards(): xb = lax.ppermute(xb, 'gx', swap(count_x, 1))  2.85 us
    ppermute x1, waiting for transfers between devices, shards(): yb = lax.ppermute(yb, 'gy', swap(count_y, 1))  2.23 us
    ppermute x1, starting transfers between devices, shards(): ya = lax.ppermute(ya, 'gy', swap(count_y, 0))  2 us
    unnamed x12, local copies, waits for them, and re-layouts  1.31 us
    ppermute x1, waiting for transfers between devices, shards(): xb = lax.ppermute(xb, 'gx', swap(count_x, 1))  1.07 us
  transfers between devices with their start and end apart: 5, of which 3 were waited for; matrix products, arithmetic and copies ran while one was open for 0% of the time, Pallas kernels for 21%

profile of v6, /device:TPU:24, one launch (start us, length us, event | category | flops | bytes accessed | tf_op | source)
XLA Modules:
  0.0 30.0 jit_solution(7257887326586232312)
XLA Ops:
  0.6 0.0 copy-start
  0.6 0.0 copy-start.1
  0.7 0.0 copy-start.2
  0.7 0.0 copy-start.3
  0.7 1.2 %constant_dynamic-update-slice_fusion.1 = f32[23,8,16,128]{3,2,1,0:T(8,128)S(1)} fusion(f32[10,8,16,128]{3,2,1,0:T(8,128)} %param.8), kind=kLoop, calls=%fused_computation.4 | loop fusion | bytes 1310720
  1.9 0.0 copy-done
  2.0 0.0 copy-done.1
  2.0 0.0 copy-done.2
  2.0 0.0 copy-done.3
  2.0 0.9 %pack.1 = (f32[8,16,128]{2,1,0:T(8,128)S(1)}, f32[8,16,128]{2,1,0:T(8,128)S(1)}, f32[8,16,128]{2,1,0:T(8,128)S(1)}, f32[8,16,128]{2,1,0:T(8,128)S(1)}) custom-call(f32[23,8,16,128]{3,2,1,0:T(8,128)S(1)} %bitcast_dynamic-update-slice_fusion.fields), custom_call_target="tpu_custom_call" | custom-call | tf_op jit(solution)/shard_map/pack/pallas_call | solution.py:465
  2.9 2.0 %collective-permute-start = (f32[8,16,128]{2,1,0:T(8,128)S(1)}, f32[8,16,128]{2,1,0:T(8,128)S(1)}, u32[]{:S(2)}, u32[]{:S(2)}) collective-permute-start(f32[8,16,128]{2,1,0:T(8,128)S(1)} %get-tuple-element.16), channel_id=1, source_target_pairs={{0,1},{1,0},{2,3},{3,2},{4,5},{5,4},{6,7},{7,6},{8,9},{9,8},{10,11... | collective-permute-start | bytes 196616 | tf_op jit(solution)/shard_map/ppermute | solution.py:472
  4.9 7.5 %collective-permute-start.1 = (f32[8,16,128]{2,1,0:T(8,128)S(1)}, f32[8,16,128]{2,1,0:T(8,128)S(1)}, u32[]{:S(2)}, u32[]{:S(2)}) collective-permute-start(f32[8,16,128]{2,1,0:T(8,128)S(1)} %get-tuple-element.17), channel_id=1, source_target_pairs={{1,2},{2,1},{3,4},{4,3},{5,6},{6,5},{7,8},{8,7},{9,10},{10,9},{11,... | collective-permute-start | bytes 196616 | tf_op jit(solution)/shard_map/ppermute | solution.py:471
  12.5 0.0 collective-permute-done.ya
  12.5 2.2 %collective-permute-done.1.yb = f32[8,16,128]{2,1,0:T(8,128)S(1)} collective-permute-done((f32[8,16,128]{2,1,0:T(8,128)S(1)}, f32[8,16,128]{2,1,0:T(8,128)S(1)}, u32[]{:S(2)}, u32[]{:S(2)}) %collective-permute-start.1) | collective-permute-done | bytes 65568 | tf_op jit(solution)/shard_map/ppermute | solution.py:471
  14.7 0.1 rows.1
  14.8 2.9 %collective-permute-start.2 = (f32[13,8,8,128]{3,2,1,0:T(8,128)S(1)}, f32[13,8,8,128]{3,2,1,0:T(8,128)S(1)}, u32[]{:S(2)}, u32[]{:S(2)}) collective-permute-start(f32[13,8,8,128]{3,2,1,0:T(8,128)S(1)} %get-tuple-element.18), channel_id=1, source_target_pairs={{16,32},{32,16},{48,64},{64,48},{80,96},{96,80},{112,128},{128,112... | collective-permute-start | bytes 1277960 | tf_op jit(solution)/shard_map/ppermute | solution.py:479
  17.7 0.1 core.1
  17.8 0.7 %collective-permute-start.3 = (f32[10,8,8,128]{3,2,1,0:T(8,128)S(1)}, f32[10,8,8,128]{3,2,1,0:T(8,128)S(1)}, u32[]{:S(2)}, u32[]{:S(2)}) collective-permute-start(f32[10,8,8,128]{3,2,1,0:T(8,128)S(1)} %get-tuple-element.22), channel_id=1, source_target_pairs={{0,16},{16,0},{32,48},{48,32},{64,80},{80,64},{96,112},{112,96},{1... | collective-permute-start | bytes 983048 | tf_op jit(solution)/shard_map/ppermute | solution.py:487
  18.5 0.1 collective-permute-start.4
  18.6 0.1 setup.1.mats
  18.7 0.6 %halo.1.hy = f32[2,8,32,128]{3,2,1,0:T(8,128)S(1)} custom-call(f32[8,16,128]{2,1,0:T(8,128)S(1)} %get-tuple-element.20.e1, f32[8,16,128]{2,1,0:T(8,128)S(1)} %get-tuple-element.21.e2, f32[8,16,128]{2,1,0:T(8,128)S(1)} %collective-permute-done.ya, f32[8,16,128]{2,1,0:T(8,128)S(1)} %collective-permute-done.1.yb), custom_call_target="tpu_custom_call" | custom-call | bytes 2097152 | tf_op jit(solution)/shard_map/halo/pallas_call | solution.py:489
  19.3 0.6 %collective-permute-done.4.xa_rest = f32[3,8,8,128]{3,2,1,0:T(8,128)S(1)} collective-permute-done((f32[3,8,8,128]{3,2,1,0:T(8,128)S(1)}, f32[3,8,8,128]{3,2,1,0:T(8,128)S(1)}, u32[]{:S(2)}, u32[]{:S(2)}) %collective-permute-start.4) | collective-permute-done | bytes 98336 | tf_op jit(solution)/shard_map/ppermute | solution.py:488
  19.9 0.0 collective-permute-done.3.xa
  19.9 5.4 %near.1 = (f32[8,16,128]{2,1,0:T(8,128)S(1)}, f32[8,16,128]{2,1,0:T(8,128)S(1)}, f32[10,8,16,128]{3,2,1,0:T(8,128)S(1)}, f32[10,8,16,128]{3,2,1,0:T(8,128)S(1)}) custom-call(bf16[12,256,128]{2,1,0:T(8,128)(2,1)S(1)} %setup.1.mats, f32[23,8,16,128]{3,2,1,0:T(8,128)S(1)} %bitcast_dynamic-update-slice_fusion.fields, ...), custom_call_target="tpu_custom_call" | custom-call | bytes 16777216 | tf_op jit(solution)/shard_map/near/pallas_call | solution.py:496
  25.3 1.1 %collective-permute-done.2.xb = f32[13,8,8,128]{3,2,1,0:T(8,128)S(1)} collective-permute-done((f32[13,8,8,128]{3,2,1,0:T(8,128)S(1)}, f32[13,8,8,128]{3,2,1,0:T(8,128)S(1)}, u32[]{:S(2)}, u32[]{:S(2)}) %collective-permute-start.2) | collective-permute-done | bytes 426016 | tf_op jit(solution)/shard_map/ppermute | solution.py:479
  26.4 3.6 %rest.1 = (f32[8,16,128]{2,1,0:T(8,128)}, f32[8,16,128]{2,1,0:T(8,128)}, f32[10,8,16,128]{3,2,1,0:T(8,128)}, f32[10,8,16,128]{3,2,1,0:T(8,128)}) custom-call(bf16[12,256,128]{2,1,0:T(8,128)(2,1)S(1)} %setup.1.mats, f32[23,8,16,128]{3,2,1,0:T(8,128)S(1)} %bitcast_dynamic-update-slice_fusion.fields, f32[13,8,8,128]{3,2,1,0:T(8,128)S(1)} %collective-permute-done.2.xb, ...), custom_call_target="tpu_custom_call" | custom-call | bytes 8388608 | tf_op jit(solution)/shard_map/rest/pallas_call | solution.py:504
  (4 shorter events, 0.1 us)
Async XLA Ops:
  0.6 1.3 %copy-start = (f32[10,8,16,128]{3,2,1,0:T(8,128)S(1)}, f32[10,8,16,128]{3,2,1,0:T(8,128)}, u32[]{:S(2)}) copy-start(f32[10,8,16,128]{3,2,1,0:T(8,128)} %param.9) | copy-start | bytes 1966084
  0.6 1.3 %copy-start.1 = (f32[8,16,128]{2,1,0:T(8,128)S(1)}, f32[8,16,128]{2,1,0:T(8,128)}, u32[]{:S(2)}) copy-start(f32[8,16,128]{2,1,0:T(8,128)} %param.5) | copy-start | bytes 196612
  0.7 1.3 %copy-start.2 = (f32[8,16,128]{2,1,0:T(8,128)S(1)}, f32[8,16,128]{2,1,0:T(8,128)}, u32[]{:S(2)}) copy-start(f32[8,16,128]{2,1,0:T(8,128)} %param.6) | copy-start | bytes 196612
  0.7 1.4 %copy-start.3 = (f32[8,16,128]{2,1,0:T(8,128)S(1)}, f32[8,16,128]{2,1,0:T(8,128)}, u32[]{:S(2)}) copy-start(f32[8,16,128]{2,1,0:T(8,128)} %param.7) | copy-start | bytes 196612
  2.9 9.5 %collective-permute-start = (f32[8,16,128]{2,1,0:T(8,128)S(1)}, f32[8,16,128]{2,1,0:T(8,128)S(1)}, u32[]{:S(2)}, u32[]{:S(2)}) collective-permute-start(f32[8,16,128]{2,1,0:T(8,128)S(1)} %get-tuple-element.16), channel_id=1, source_target_pairs={{0,1},{1,0},{2,3},{3,2},{4,5},{5,4},{6,7},{7,6},{8,9},{9,8},{10,11... | collective-permute-start | bytes 196616 | tf_op jit(solution)/shard_map/ppermute | solution.py:472
  4.9 9.8 %collective-permute-start.1 = (f32[8,16,128]{2,1,0:T(8,128)S(1)}, f32[8,16,128]{2,1,0:T(8,128)S(1)}, u32[]{:S(2)}, u32[]{:S(2)}) collective-permute-start(f32[8,16,128]{2,1,0:T(8,128)S(1)} %get-tuple-element.17), channel_id=1, source_target_pairs={{1,2},{2,1},{3,4},{4,3},{5,6},{6,5},{7,8},{8,7},{9,10},{10,9},{11,... | collective-permute-start | bytes 196616 | tf_op jit(solution)/shard_map/ppermute | solution.py:471
  14.8 11.6 %collective-permute-start.2 = (f32[13,8,8,128]{3,2,1,0:T(8,128)S(1)}, f32[13,8,8,128]{3,2,1,0:T(8,128)S(1)}, u32[]{:S(2)}, u32[]{:S(2)}) collective-permute-start(f32[13,8,8,128]{3,2,1,0:T(8,128)S(1)} %get-tuple-element.18), channel_id=1, source_target_pairs={{16,32},{32,16},{48,64},{64,48},{80,96},{96,80},{112,128},{128,112... | collective-permute-start | bytes 1277960 | tf_op jit(solution)/shard_map/ppermute | solution.py:479
  17.8 2.1 %collective-permute-start.3 = (f32[10,8,8,128]{3,2,1,0:T(8,128)S(1)}, f32[10,8,8,128]{3,2,1,0:T(8,128)S(1)}, u32[]{:S(2)}, u32[]{:S(2)}) collective-permute-start(f32[10,8,8,128]{3,2,1,0:T(8,128)S(1)} %get-tuple-element.22), channel_id=1, source_target_pairs={{0,16},{16,0},{32,48},{48,32},{64,80},{80,64},{96,112},{112,96},{1... | collective-permute-start | bytes 983048 | tf_op jit(solution)/shard_map/ppermute | solution.py:487
  18.5 1.4 %collective-permute-start.4 = (f32[3,8,8,128]{3,2,1,0:T(8,128)S(1)}, f32[3,8,8,128]{3,2,1,0:T(8,128)S(1)}, u32[]{:S(2)}, u32[]{:S(2)}) collective-permute-start(f32[3,8,8,128]{3,2,1,0:T(8,128)S(1)} %get-tuple-element.23), channel_id=1, source_target_pairs={{0,16},{16,0},{32,48},{48,32},{64,80},{80,64},{96,112},{112,96},{1... | collective-permute-start | bytes 294920 | tf_op jit(solution)/shard_map/ppermute | solution.py:488
